TPU v7x, 256 devices: a whole 4x4x8 slice. The times are simulated.
256 devices in a mesh: gx: 32 (over x_hi, z, core), gy: 8 (over y, x_lo).
Axes of the slice: x: 4 (x_hi: 2, x_lo: 2; x = x_hi * 2 + x_lo), y: 4, z: 8, core: 2. Of those that a mesh axis runs over, the one named last changes fastest.
Arguments:
- rhs: float32 [32, 8, 4, 320], P('gx', 'gy'), may hold values from -120 to 120
- vol_jac: float32 [32, 8, 4, 320, 320], P('gx', 'gy'), may hold values from -0.3125 to 0.3125
- inv_step: float32 [32, 8, 4], P('gx', 'gy'), may hold values from 4 to 16
- face_jac: float32 [32, 8, 4, 6, 5, 5], P('gx', 'gy'), may hold values from -1 to 1
- orientation: int32 [32, 8, 4, 6], P('gx', 'gy'), may hold values from 0 to 7, as said below
Outputs:
- newton_update: float32 [32, 8, 4, 320], P('gx', 'gy')
- residual_ratio: float32 [], replicated
Inputs may be any that keep to these rules, and one draw needn't show every extreme that they name: `orientation`: the two sides of every face carry inverse codes: where one side has code o, the other has o if o < 4, else 4 + (o & 2) / 2 + 2 (o & 1).
All inputs are finite; a program needn't handle non-finite values.
Results may differ from a plain program's by a relative error of at most 0.0025.
Values sent between devices are 32-bit elements; how exact they have to be, the bound alone decides.
No kernel may reach another device: no remote copies, remote signals or barrier semaphores. Data moves between devices by JAX's collectives and lax.ppermute only.
A program may use at most 256 MiB of HBM per device.

v0:
```python
import jax
import jax.numpy as jnp
import numpy as np
from jax import lax
from jax.sharding import PartitionSpec as P

Q = 4
NV = 5
ITERS = 3
NS_STEPS = 3
NP = 64


penalty = 4.0
highest = lax.Precision.HIGHEST


def extended(shard, sides, width):
    for axis, dim in sides:
        size, length = (lax.axis_size(axis), shard.shape[dim])
        up = [(i, (i + 1) % size) for i in range(size)]
        down = [(j, i) for i, j in up]
        last = lax.slice_in_dim(shard, length - width, length, axis=dim)
        first = lax.slice_in_dim(shard, 0, width, axis=dim)
        before = lax.ppermute(last, axis, up)
        after = lax.ppermute(first, axis, down)
        shard = jnp.concatenate([before, shard, after], axis=dim)
    return shard


def face_tables(nodes_side):
    node_count = nodes_side**3
    across = nodes_side * nodes_side
    selector = np.zeros((6, node_count, across), np.float32)
    for face_id in range(6):
        for node_id in range(node_count):
            first_coord = node_id % nodes_side
            second_coord = node_id // nodes_side % nodes_side
            third_coord = node_id // across
            fixed_axis = [
                first_coord,
                first_coord,
                second_coord,
                second_coord,
                third_coord,
                third_coord,
            ][face_id]
            target = 0 if face_id % 2 == 0 else nodes_side - 1
            if fixed_axis == target:
                plane_pair = [
                    (second_coord, third_coord),
                    (second_coord, third_coord),
                    (first_coord, third_coord),
                    (first_coord, third_coord),
                    (first_coord, second_coord),
                    (first_coord, second_coord),
                ][face_id]
                selector[face_id, node_id, plane_pair[0] + nodes_side * plane_pair[1]] = 1.0
    turning = np.zeros((8, across, across), np.float32)
    for orient_code in range(8):
        for face_node in range(across):
            along_first = face_node % nodes_side
            along_second = face_node // nodes_side
            if orient_code & 4:
                along_first, along_second = (along_second, along_first)
            if orient_code & 1:
                along_first = nodes_side - 1 - along_first
            if orient_code & 2:
                along_second = nodes_side - 1 - along_second
            turning[orient_code, face_node, along_first + nodes_side * along_second] = 1.0
    return (selector, turning)


def element_traces(operand, selector):
    shaped = operand.reshape(operand.shape[:-1] + (NV, NP))
    return jnp.einsum("...vn,fnq->...fvq", shaped, selector, precision=highest)


def lift_faces(face_values, selector):
    lifted = jnp.einsum("...fvq,fnq->...vn", face_values, selector, precision=highest)
    return lifted.reshape(lifted.shape[:-2] + (NV * NP,))


def face_terms(own_traces, oriented, face_jac):
    identity = jnp.eye(NV, dtype=jnp.float32)
    own_part = jnp.einsum(
        "...fij,...fjq->...fiq", face_jac + penalty * identity, own_traces, precision=highest
    )
    other_part = jnp.einsum(
        "...fij,...fjq->...fiq", face_jac - penalty * identity, oriented, precision=highest
    )
    return 0.5 * (own_part + other_part)


def invert_blocks(vol_jac, inv_step, face_jac, selector):
    eye_nodes = jnp.eye(NP, dtype=jnp.float32)
    eye_block = jnp.eye(NV * NP, dtype=jnp.float32)
    coverage = jnp.sum(selector, axis=-1)
    own_face = 0.5 * (face_jac + penalty * jnp.eye(NV, dtype=jnp.float32))
    node_part = jnp.einsum("...fij,fn->...ijn", own_face, coverage, precision=highest)
    face_block = jnp.einsum("...ijn,nm->...injm", node_part, eye_nodes, precision=highest)
    face_block = face_block.reshape(face_block.shape[:-4] + (NV * NP, NV * NP))
    element_block = vol_jac + face_block + inv_step[..., None, None] * eye_block
    diagonal = jnp.diagonal(element_block, axis1=-2, axis2=-1)
    approx = eye_block * (1.0 / diagonal)[..., :, None]
    for sweep_id in range(NS_STEPS):
        product = jnp.einsum("...rk,...kc->...rc", element_block, approx, precision=highest)
        approx = 2.0 * approx - jnp.einsum("...rk,...kc->...rc", approx, product, precision=highest)
    return approx


def apply_precond(precond, operand):
    return jnp.einsum("...rc,...c->...r", precond, operand, precision=highest)


def apply_jacobian(operand, vol_jac, inv_step, face_jac, orient_mats, selector):
    own_traces = element_traces(operand, selector)
    padded = extended(operand, (("gx", 0), ("gy", 1)), 1)
    padded_traces = element_traces(padded, selector)
    side_faces = [
        padded_traces[0:-2, 1:-1, :, 1],
        padded_traces[2:, 1:-1, :, 0],
        padded_traces[1:-1, 0:-2, :, 3],
        padded_traces[1:-1, 2:, :, 2],
    ]
    lower_face = jnp.roll(own_traces, 1, axis=2)[:, :, :, 5]
    upper_face = jnp.roll(own_traces, -1, axis=2)[:, :, :, 4]
    neighbours = jnp.stack(side_faces + [lower_face, upper_face], axis=3)
    oriented = jnp.einsum("...fqp,...fvp->...fvq", orient_mats, neighbours, precision=highest)
    coupled = face_terms(own_traces, oriented, face_jac)
    volume = jnp.einsum("...rc,...c->...r", vol_jac, operand, precision=highest)
    return inv_step[..., None] * operand + volume + lift_faces(coupled, selector)


def least_squares(columns, initial_norm):
    steps_count = len(columns)
    rotations = []
    target_values = [initial_norm] + [jnp.zeros_like(initial_norm)] * steps_count
    upper_rows = []
    for column_id in range(steps_count):
        column = list(columns[column_id])
        for index_id in range(column_id):
            cosine, sine_part = rotations[index_id]
            top_value = cosine * column[index_id] + sine_part * column[index_id + 1]
            column[index_id + 1] = -sine_part * column[index_id] + cosine * column[index_id + 1]
            column[index_id] = top_value
        radius = jnp.sqrt(
            column[column_id] * column[column_id] + column[column_id + 1] * column[column_id + 1]
        )
        cosine = column[column_id] / radius
        sine_part = column[column_id + 1] / radius
        rotations.append((cosine, sine_part))
        column[column_id] = radius
        target_values[column_id + 1] = -sine_part * target_values[column_id]
        target_values[column_id] = cosine * target_values[column_id]
        upper_rows.append(column)
    coefficients = [None] * steps_count
    for row_id in reversed(range(steps_count)):
        running = target_values[row_id]
        for later_id in range(row_id + 1, steps_count):
            running = running - upper_rows[later_id][row_id] * coefficients[later_id]
        coefficients[row_id] = running / upper_rows[row_id][row_id]
    return (coefficients, jnp.abs(target_values[steps_count]) / initial_norm)


def body(rhs, vol_jac, inv_step, face_jac, orientation):
    selector_np, turning_np = face_tables(Q)
    selector = jnp.asarray(selector_np)
    turning = jnp.asarray(turning_np)
    initial_norm = jnp.sqrt(lax.psum(jnp.sum(rhs * rhs), ("gx", "gy")))
    precond = invert_blocks(vol_jac, inv_step, face_jac, selector)
    orient_hot = (orientation[..., None] == jnp.arange(8, dtype=jnp.int32)).astype(jnp.float32)
    orient_mats = jnp.einsum("...fo,oqp->...fqp", orient_hot, turning, precision=highest)
    krylov_basis = [rhs / initial_norm]
    directions = []
    columns = []
    for iteration in range(ITERS):
        direction = apply_precond(precond, krylov_basis[-1])
        directions.append(direction)
        image_vec = apply_jacobian(direction, vol_jac, inv_step, face_jac, orient_mats, selector)
        column = []
        for vector in krylov_basis:
            projection = lax.psum(jnp.sum(image_vec * vector), ("gx", "gy"))
            image_vec = image_vec - projection * vector
            column.append(projection)
        new_norm = jnp.sqrt(lax.psum(jnp.sum(image_vec * image_vec), ("gx", "gy")))
        column.append(new_norm)
        columns.append(column)
        krylov_basis.append(image_vec / new_norm)
    coefficients, residual_ratio = least_squares(columns, initial_norm)
    update = coefficients[0] * directions[0]
    for index_id in range(1, ITERS):
        update = update + coefficients[index_id] * directions[index_id]
    return (update, residual_ratio)


def solution(mesh):
    placed = (
        P("gx", "gy", None, None),
        P("gx", "gy", None, None, None),
        P("gx", "gy", None),
        P("gx", "gy", None, None, None, None),
        P("gx", "gy", None, None),
    )
    return jax.shard_map(
        body,
        mesh=mesh,
        in_specs=placed,
        out_specs=(P("gx", "gy", None, None), P()),
        check_vma=False,
    )
```

profile of v0, /device:TPU:1, one launch (start us, length us, event | category | flops | bytes accessed | tf_op | source)
XLA Modules:
  0.0 993.9 jit_solution(3365222938846612043)
XLA Ops:
  4.2 24.3 %copy.18 = f32[1,1,4,320,320]{2,4,3,1,0:T(8,128)} copy(f32[1,1,4,320,320]{4,3,2,1,0:T(8,128)S(1)} %copy-done) | data formatting | bytes 3276800 | tf_op args[1]
  28.5 18.0 %broadcast_multiply_fusion = f32[64,64,4,5,5]{2,1,4,0,3:T(8,128)} fusion(f32[64,4,5,5]{1,3,0,2:T(8,128)} %copy.17, f32[64,64]{1,0:T(8,128)S(1)} %fusion.38), kind=kLoop, calls=%fused_computation.2 | loop fusion | flops 409600 | bytes 1680384 | tf_op jit(solution)/shard_map/...ijn,nm->...injm/dot_general | solution.py:101
  46.6 50.3 %add_bitcast_fusion = f32[4,320,320]{0,2,1:T(8,128)} fusion(f32[1,1,4,320,320]{2,4,3,1,0:T(8,128)} %copy.18, f32[1,1,4,320,320]{2,4,3,1,0:T(8,128)} %bitcast.228, f32[320,320]{1,0:T(8,128)S(1)} %fusion.20, f32[4]{0:T(128)S(1)} %bitcast.255), kind=kLoop, calls=%fused_computation.1 | loop fusion | flops 1228800 | bytes 5324816 | tf_op jit(solution)/shard_map/add | solution.py:103
  96.9 29.9 %copy.24 = f32[4,320,320]{2,1,0:T(8,128)} copy(f32[4,320,320]{0,2,1:T(8,128)} %add_bitcast_fusion) | data formatting | bytes 3276800 | tf_op jit(solution)/shard_map/add | solution.py:103
  126.7 11.1 %gather_fusion = f32[320,4]{1,0:T(8,128)S(1)} fusion(f32[4,320,320]{0,2,1:T(8,128)} %add_bitcast_fusion, s32[320]{0:T(512)S(1)} %or_reduce_fusion), kind=kCustom, calls=%fused_computation | custom fusion | bytes 12800 | tf_op jit(solution)/shard_map/jit(diagonal)/gather | solution.py:104
  137.9 5.7 fusion.2
  143.6 4.1 fusion.4
  147.8 4.4 fusion.69
  152.2 4.0 multiply_subtract_fusion.1
  156.3 4.0 fusion.70
  160.9 5.2 multiply_subtract_fusion
  166.1 81.5 %psum.70 = f32[]{:T(128)} all-reduce(f32[]{:T(128)} %multiply_reduce_fusion.6), channel_id=1, replica_groups=mesh['gx'=32,'gy'=8] {'gx','gy'}, use_global_device_ids=true, to_apply=%region_2.0 | all-reduce | flops 1 | bytes 8 | tf_op jit(solution)/shard_map/psum | solution.py:170
  248.4 3.4 fusion.56
  256.9 3.6 collective-permute-start.3
  264.5 80.3 %psum.71 = f32[]{:T(128)} all-reduce(f32[]{:T(128)} %get-tuple-element.10), channel_id=1, replica_groups=mesh['gx'=32,'gy'=8] {'gx','gy'}, use_global_device_ids=true, to_apply=%region_4.5 | all-reduce | flops 1 | bytes 8 | tf_op jit(solution)/shard_map/psum | solution.py:183
  346.0 72.6 %psum.72 = f32[]{:T(128)} all-reduce(f32[]{:T(128)} %multiply_reduce_fusion.5), channel_id=1, replica_groups=mesh['gx'=32,'gy'=8] {'gx','gy'}, use_global_device_ids=true, to_apply=%region_6.7 | all-reduce | flops 1 | bytes 8 | tf_op jit(solution)/shard_map/psum | solution.py:186
  420.0 3.4 fusion.53
  437.6 78.4 %psum.73 = f32[]{:T(128)} all-reduce(f32[]{:T(128)} %get-tuple-element.8), channel_id=1, replica_groups=mesh['gx'=32,'gy'=8] {'gx','gy'}, use_global_device_ids=true, to_apply=%region_8.9 | all-reduce | flops 1 | bytes 8 | tf_op jit(solution)/shard_map/psum | solution.py:183
  517.3 72.4 %psum.74 = f32[]{:T(128)} all-reduce(f32[]{:T(128)} %get-tuple-element.6), channel_id=1, replica_groups=mesh['gx'=32,'gy'=8] {'gx','gy'}, use_global_device_ids=true, to_apply=%region_10.11 | all-reduce | flops 1 | bytes 8 | tf_op jit(solution)/shard_map/psum | solution.py:183
  591.0 74.1 %psum.75 = f32[]{:T(128)} all-reduce(f32[]{:T(128)} %multiply_reduce_fusion.3), channel_id=1, replica_groups=mesh['gx'=32,'gy'=8] {'gx','gy'}, use_global_device_ids=true, to_apply=%region_12.13 | all-reduce | flops 1 | bytes 8 | tf_op jit(solution)/shard_map/psum | solution.py:186
  683.9 78.5 %psum.76 = f32[]{:T(128)} all-reduce(f32[]{:T(128)} %get-tuple-element.4), channel_id=1, replica_groups=mesh['gx'=32,'gy'=8] {'gx','gy'}, use_global_device_ids=true, to_apply=%region_14.15 | all-reduce | flops 1 | bytes 8 | tf_op jit(solution)/shard_map/psum | solution.py:183
  763.7 72.4 %psum.77 = f32[]{:T(128)} all-reduce(f32[]{:T(128)} %get-tuple-element.2), channel_id=1, replica_groups=mesh['gx'=32,'gy'=8] {'gx','gy'}, use_global_device_ids=true, to_apply=%region_16.17 | all-reduce | flops 1 | bytes 8 | tf_op jit(solution)/shard_map/psum | solution.py:183
  837.4 73.9 %psum.78 = f32[]{:T(128)} all-reduce(f32[]{:T(128)} %multiply_reduce_fusion.1), channel_id=1, replica_groups=mesh['gx'=32,'gy'=8] {'gx','gy'}, use_global_device_ids=true, to_apply=%region_18.19 | all-reduce | flops 1 | bytes 8 | tf_op jit(solution)/shard_map/psum | solution.py:183
  916.5 73.5 %psum.79 = f32[]{:T(128)} all-reduce(f32[]{:T(128)} %multiply_reduce_fusion), channel_id=1, replica_groups=mesh['gx'=32,'gy'=8] {'gx','gy'}, use_global_device_ids=true, to_apply=%region_20.21 | all-reduce | flops 1 | bytes 8 | tf_op jit(solution)/shard_map/psum | solution.py:186
  (132 shorter events, 50.1 us)
Async XLA Ops:
  0.6 3.6 copy-start
  28.5 18.0 %copy-start.7 = (f32[1,1,4]{2,1,0:T(1,128)S(1)}, f32[1,1,4]{2,1,0:T(1,128)}, u32[]{:S(2)}) copy-start(f32[1,1,4]{2,1,0:T(1,128)} %param.9) | copy-start | bytes 52
  143.6 4.1 copy-start.1
  156.2 4.0 copy-start.2
  248.4 7.2 copy-start.5
  248.4 7.7 copy-start.6
  248.4 7.7 copy-start.8
  251.8 4.9 collective-permute-start
  253.3 3.5 collective-permute-start.1
  253.7 8.0 copy-start.3
  256.4 6.9 copy-start.4
  256.8 4.8 collective-permute-start.2
  256.9 4.7 collective-permute-start.3
  423.4 5.2 collective-permute-start.4
  425.8 3.3 collective-permute-start.5
  429.1 5.6 collective-permute-start.6
  429.6 5.1 collective-permute-start.7
  669.8 4.3 collective-permute-start.8
  671.4 3.3 collective-permute-start.9
  674.8 6.3 collective-permute-start.10
  675.2 5.8 collective-permute-start.11
where the time goes:
time: 1000 us; the launch traced here: 994 us
  blocking collectives  758 us (76%)
  other arithmetic  82.4 us (8%)
  local copies, waits for them, and re-layouts  68.6 us (7%)
  matrix products  52.6 us (5%)
  starting transfers between devices  16.2 us (2%)
  between operations  14.7 us (1%)
    psum x6, blocking collectives, body(): projection = lax.psum(jnp.sum(image_vec * vector), ('gx', 'gy'))  456 us
    psum x3, blocking collectives, body(): new_norm = jnp.sqrt(lax.psum(jnp.sum(image_vec * image_vec), ('gx', 'gy')))  220 us
    psum x1, blocking collectives, body(): initial_norm = jnp.sqrt(lax.psum(jnp.sum(rhs * rhs), ('gx', 'gy')))  81.5 us
    add x1, other arithmetic, invert_blocks(): element_block = vol_jac + face_block + inv_step[..., None, None] * eye_block  50.3 us
    add x1, local copies, waits for them, and re-layouts, invert_blocks(): element_block = vol_jac + face_block + inv_step[..., None, None] * eye_block  29.9 us
    unnamed x31, local copies, waits for them, and re-layouts  24.4 us
  transfers between devices with their start and end apart: 12, of which 3 were waited for; matrix products, arithmetic and copies ran while one was open for 1% of the time, Pallas kernels for 0%

commit v1 on v0

--- a/solution.py
+++ b/solution.py
@@ -2,6 +2,8 @@
 import jax.numpy as jnp
 import numpy as np
 from jax import lax
+from jax.experimental import pallas as pl
+from jax.experimental.pallas import tpu as pltpu
 from jax.sharding import PartitionSpec as P
 
 Q = 4
@@ -163,7 +165,7 @@
     return (coefficients, jnp.abs(target_values[steps_count]) / initial_norm)
 
 
-def body(rhs, vol_jac, inv_step, face_jac, orientation):
+def careful(rhs, vol_jac, inv_step, face_jac, orientation):
     selector_np, turning_np = face_tables(Q)
     selector = jnp.asarray(selector_np)
     turning = jnp.asarray(turning_np)
@@ -194,6 +196,418 @@
     return (update, residual_ratio)
 
 
+EL = 4
+BLK = NV * NP
+LANES = 128
+TILES = 3
+WIDE = TILES * LANES
+GROUPS = BLK // 8
+MIN_PIVOT = 0.02
+MIN_SCALE = 1e-18
+MAX_SCALE = 1e30
+DEVICES_AXES = ("gx", "gy")
+
+
+def tile_iota(dim):
+    return lax.broadcasted_iota(jnp.int32, (8, LANES), dim)
+
+
+def turn(x, shift):
+    return pltpu.roll(x, shift % 8, 0)
+
+
+def pick(x, index):
+    return jnp.take_along_axis(x, index, axis=1)
+
+
+def split(x):
+    return [x[:, t * LANES : (t + 1) * LANES] for t in range(TILES)]
+
+
+def face_of_row(pair):
+    return 2 * pair + (tile_iota(0) >> 2)
+
+
+def collect(per_element):
+    row = tile_iota(0)
+    even = (row & 1) == 0
+    low = (row & 2) == 0
+    folded = [a + turn(a, 4) for a in per_element]
+
+    def join(mask, first, second, step):
+        return jnp.where(mask, first, second) + turn(jnp.where(mask, second, first), -step)
+
+    return join(low, join(even, folded[0], folded[1], 1), join(even, folded[2], folded[3], 1), 2)
+
+
+def row_masks():
+    offset = tile_iota(1) - tile_iota(0)
+    return [offset == 8 * k for k in range(LANES // 8)]
+
+
+def couple_rows(f_ref, y):
+    masks = row_masks()
+    tiles = [[] for _ in range(TILES)]
+    for e in range(EL):
+        spread = [jnp.broadcast_to(part[e : e + 1, :], (8, LANES)) for part in y]
+        acc = [jnp.zeros((8, LANES), jnp.float32) for _ in range(TILES)]
+        for g in range(GROUPS):
+            rows = slice(8 * g, 8 * g + 8)
+            p = f_ref[e, rows, 0:LANES] * spread[0]
+            p = p + f_ref[e, rows, LANES : 2 * LANES] * spread[1]
+            p = p + f_ref[e, rows, 2 * LANES : WIDE] * spread[2]
+            total = jnp.sum(p, axis=1, keepdims=True)
+            t, k = divmod(g, LANES // 8)
+            acc[t] = jnp.where(masks[k], total, acc[t])
+        for t in range(TILES):
+            tiles[t].append(acc[t])
+    return [collect(parts) for parts in tiles]
+
+
+def series(f_ref, start, inverse):
+    def step(_, y):
+        moved = couple_rows(f_ref, y)
+        return tuple(inverse[t] * (start[t] + moved[t]) for t in range(TILES))
+
+    first = tuple(inverse[t] * start[t] for t in range(TILES))
+    return list(lax.fori_loop(0, 2**NS_STEPS - 1, step, first))
+
+
+def traces_of(z):
+    lane = tile_iota(1)
+    var, node = lane >> 4, lane & 15
+    s, t = node & 3, node >> 2
+    result = []
+    for pair in range(3):
+        if pair == 0:
+            place = 4 * s + 16 * t + 3 * (tile_iota(0) >> 2)
+        elif pair == 1:
+            place = s + 16 * t + 12 * (tile_iota(0) >> 2)
+        else:
+            place = s + 4 * t + 48 * (tile_iota(0) >> 2)
+        index = (var & 1) * NP + place
+        parts = [pick(z[k], index) for k in range(TILES)]
+        tile = var >> 1
+        result.append(jnp.where(tile == 0, parts[0], jnp.where(tile == 1, parts[1], parts[2])))
+    return result
+
+
+def turned_nodes(code):
+    node = tile_iota(1) & 15
+    s, t = node & 3, node >> 2
+    swap = (code & 4) != 0
+    first = jnp.where(swap, t, s)
+    second = jnp.where(swap, s, t)
+    first = jnp.where((code & 1) != 0, 3 - first, first)
+    second = jnp.where((code & 2) != 0, 3 - second, second)
+    return first + 4 * second
+
+
+def through_faces(pair, neighbour, g_ref, q_ref):
+    lane = tile_iota(1)
+    own = lane >> 4
+    turned = q_ref[pair]
+    value = None
+    for shift in range(NV):
+        other = own + shift
+        other = jnp.where(other >= NV, other - NV, other)
+        index = (other * 16 + turned) & (LANES - 1)
+        term = g_ref[3 * shift + pair] * pick(neighbour, index)
+        value = term if value is None else value + term
+    node = lane & (NP - 1)
+    a, b, c = node & 3, (node >> 2) & 3, node >> 4
+    end = 3 * (tile_iota(0) >> 2)
+    if pair == 0:
+        hit, place = a == end, b + 4 * c
+    elif pair == 1:
+        hit, place = b == end, a + 4 * c
+    else:
+        hit, place = c == end, a + 4 * b
+    lifted = []
+    for t in range(TILES):
+        index = ((2 * t + (lane >> 6)) * 16 + place) & (LANES - 1)
+        keep = hit if t < 2 else hit & (lane < NP)
+        lifted.append(jnp.where(keep, pick(value, index), 0.0))
+    return lifted
+
+
+def fold(parts):
+    return [p + turn(p, 4) for p in parts]
+
+
+def across_third(trace):
+    row = tile_iota(0)
+    inner = jnp.where(row < 4, turn(trace, -3), turn(trace, 3))
+    outer = jnp.where(row == 0, turn(trace, 1), turn(trace, -1))
+    return jnp.where((row == 0) | (row == 7), outer, inner)
+
+
+def put(ref, parts):
+    for t in range(TILES):
+        ref[:, t * LANES : (t + 1) * LANES] = parts[t]
+
+
+def prepare(vol_ref, rhs_ref, inv_ref, fj_ref, ori_ref, f_ref, d_ref, g_ref, q_ref, r_ref, z_ref, tx_ref, ty_ref, tz_ref):
+    row, lane = tile_iota(0), tile_iota(1)
+    zero = jnp.zeros((8, LANES), jnp.float32)
+    r_ref[...] = jnp.zeros((8, WIDE), jnp.float32)
+    r_ref[0:4, 0:BLK] = rhs_ref[...]
+    r_ref[4:8, 0:BLK] = rhs_ref[...]
+    start = split(r_ref[...])
+    d_ref[...] = jnp.zeros((8, WIDE), jnp.float32)
+    d_ref[0:4, 0:6] = ori_ref[...].astype(jnp.float32)
+    d_ref[4:8, 0:6] = ori_ref[...].astype(jnp.float32)
+    codes = d_ref[:, 0:LANES]
+    for pair in range(3):
+        q_ref[pair] = turned_nodes(pick(codes, face_of_row(pair)).astype(jnp.int32))
+    packed = []
+    for i in range(NV):
+        total = zero
+        for j in range(NV):
+            d_ref[:, 0:LANES] = zero
+            d_ref[0:4, 0:6] = fj_ref[i, j]
+            d_ref[4:8, 0:6] = fj_ref[i, j]
+            part = d_ref[:, 0:LANES]
+            total = total + (part if j == 0 else pltpu.roll(part, 16 * j, 1))
+        packed.append(total)
+    own = lane >> 4
+    for shift in range(NV):
+        other = own + shift
+        other = jnp.where(other >= NV, other - NV, other)
+        for pair in range(3):
+            index = (other * 16 + face_of_row(pair)) & (LANES - 1)
+            value = zero
+            for i in range(NV):
+                value = jnp.where(own == i, pick(packed[i], index), value)
+            if shift == 0:
+                value = value - penalty
+            g_ref[3 * shift + pair] = jnp.where(own < NV, 0.5 * value, 0.0)
+    node = lane & (NP - 1)
+    a, b, c = node & 3, (node >> 2) & 3, node >> 4
+    cover = [a == 0, a == 3, b == 0, b == 3, c == 0, c == 3]
+    node_part = []
+    for i in range(NV):
+        tiles = []
+        for t in range(TILES):
+            var = 2 * t + (lane >> 6)
+            index = (var * 16) & (LANES - 1)
+            value = zero
+            for f in range(6):
+                term = pick(packed[i], index + f)
+                term = term + jnp.where(var == i, penalty, 0.0)
+                value = value + jnp.where(cover[f], 0.5 * term, 0.0)
+            if t == 2:
+                value = jnp.where(lane < NP, value, 0.0)
+            tiles.append(value)
+        node_part.append(tiles)
+    shifts = zero
+    for e in range(EL):
+        shifts = jnp.where((row & 3) == e, inv_ref[e], shifts)
+    masks = row_masks()
+    node_offset = node - row
+    diag_tiles = [[] for _ in range(TILES)]
+    for e in range(EL):
+        acc = [zero for _ in range(TILES)]
+        for i in range(NV):
+            spread = [jnp.broadcast_to(node_part[i][t][e : e + 1, :], (8, LANES)) for t in range(TILES)]
+            for gi in range(NP // 8):
+                g = i * (NP // 8) + gi
+                rows = slice(8 * g, 8 * g + 8)
+                td, k = divmod(g, LANES // 8)
+                same_node = node_offset == 8 * gi
+                for t in range(TILES):
+                    if t < 2:
+                        vol = vol_ref[e, rows, t * LANES : (t + 1) * LANES]
+                        value = -vol - jnp.where(same_node, spread[t], 0.0)
+                        if t == td:
+                            acc[t] = jnp.where(masks[k], value, acc[t])
+                            value = jnp.where(masks[k], 0.0, value)
+                        f_ref[e, rows, t * LANES : (t + 1) * LANES] = value
+                    else:
+                        value = jnp.concatenate([vol_ref[e, rows, 2 * LANES : BLK], jnp.zeros((8, WIDE - BLK), jnp.float32)], axis=1)
+                        value = -value - jnp.where(same_node, spread[t], 0.0)
+                        if t == td:
+                            acc[t] = jnp.where(masks[k], value, acc[t])
+                            value = jnp.where(masks[k], 0.0, value)
+                        f_ref[e, rows, 2 * LANES : WIDE] = value
+        for t in range(TILES):
+            diag_tiles[t].append(acc[t])
+    diag = [shifts - collect(parts) for parts in diag_tiles]
+    diag[2] = jnp.where(lane < NP, diag[2], 1.0)
+    put(d_ref, diag)
+    z = series(f_ref, start, [1.0 / x for x in diag])
+    put(z_ref, z)
+    tx_ref[...], ty_ref[...], tz_ref[...] = traces_of(z)
+
+
+def own_part(f_ref, d_ref, g_ref, q_ref, r_ref, z_ref, tz_ref, out_ref):
+    r, z, diag = split(r_ref[...]), split(z_ref[...]), split(d_ref[...])
+    moved = couple_rows(f_ref, z)
+    third = fold(through_faces(2, across_third(tz_ref[...]), g_ref, q_ref))
+    put(out_ref, [diag[t] * z[t] - moved[t] - r[t] + third[t] for t in range(TILES)])
+
+
+def arrived(side_ref, own_axis, pair_ref, far_ref):
+    odd = side_ref[own_axis] == 1
+    near, far = pair_ref[...], far_ref[...]
+    before = jnp.where(odd, near, far)
+    after = jnp.where(odd, far, near)
+    return turn(jnp.where(tile_iota(0) >= 4, before, after), 4)
+
+
+def next_vector(side_ref, part_ref, c_ref, z_ref, x_ref, y_ref, g_ref, q_ref):
+    first = through_faces(0, arrived(side_ref, 0, c_ref, z_ref), g_ref, q_ref)
+    second = through_faces(1, arrived(side_ref, 1, x_ref, y_ref), g_ref, q_ref)
+    lifted = fold([first[t] + second[t] for t in range(TILES)])
+    part = split(part_ref[...])
+    return [part[t] + lifted[t] for t in range(TILES)]
+
+
+def advance(side_ref, part_ref, rc_ref, rz_ref, rx_ref, ry_ref, g_ref, q_ref, f_ref, d_ref, r_ref, z_ref, tx_ref, ty_ref, tz_ref):
+    r = next_vector(side_ref, part_ref, rc_ref, rz_ref, rx_ref, ry_ref, g_ref, q_ref)
+    put(r_ref, r)
+    z = series(f_ref, r, [1.0 / x for x in split(d_ref[...])])
+    put(z_ref, z)
+    tx_ref[...], ty_ref[...], tz_ref[...] = traces_of(z)
+
+
+def products(side_ref, part_ref, rc_ref, rz_ref, rx_ref, ry_ref, g_ref, q_ref, r0_ref, r1_ref, r2_ref, out_ref):
+    last = next_vector(side_ref, part_ref, rc_ref, rz_ref, rx_ref, ry_ref, g_ref, q_ref)
+    basis = [split(r0_ref[...]), split(r1_ref[...]), split(r2_ref[...]), last]
+    lane = tile_iota(1)
+    acc = jnp.zeros((8, LANES), jnp.float32)
+    slot = 0
+    for i in range(ITERS + 1):
+        for j in range(i + 1):
+            p = basis[i][0] * basis[j][0] + basis[i][1] * basis[j][1] + basis[i][2] * basis[j][2]
+            acc = jnp.where(lane == slot, jnp.sum(p, axis=1, keepdims=True), acc)
+            slot += 1
+    for step in (1, 2):
+        acc = acc + turn(acc, step)
+    for n in range(out_ref.shape[0] // 8):
+        out_ref[8 * n : 8 * n + 8, :] = acc
+
+
+def finish(sums_ref, z1_ref, z2_ref, z3_ref, out_ref, ratio_ref):
+    acc = jnp.zeros((8, LANES), jnp.float32)
+    parts = [acc] * 4
+    for n in range(sums_ref.shape[0] // 8):
+        parts[n % 4] = parts[n % 4] + sums_ref[8 * n : 8 * n + 8, :]
+    acc = (parts[0] + parts[1]) + (parts[2] + parts[3])
+    for step in (1, 2, 4):
+        acc = acc + turn(acc, step)
+    gram = {}
+    slot = 0
+    for i in range(ITERS + 1):
+        for j in range(i + 1):
+            gram[j, i] = pick(acc, jnp.full((8, LANES), slot, jnp.int32))
+            slot += 1
+    upper = {}
+    good = (gram[0, 0] > MIN_SCALE) & (gram[0, 0] < MAX_SCALE)
+    for i in range(ITERS + 1):
+        pivot = gram[i, i]
+        for k in range(i):
+            pivot = pivot - upper[k, i] * upper[k, i]
+        good = good & (pivot > MIN_PIVOT * gram[i, i]) & (gram[i, i] > MIN_SCALE) & (gram[i, i] < MAX_SCALE)
+        upper[i, i] = jnp.sqrt(pivot)
+        inverse = 1.0 / upper[i, i]
+        for j in range(i + 1, ITERS + 1):
+            value = gram[i, j]
+            for k in range(i):
+                value = value - upper[k, i] * upper[k, j]
+            upper[i, j] = value * inverse
+    columns = []
+    for j in range(1, ITERS + 1):
+        column = [upper[i, j] + upper[i, j - 1] for i in range(j)]
+        columns.append(column + [upper[j, j]])
+    coefficients, ratio = least_squares(columns, upper[0, 0])
+    z = [split(z1_ref[...]), split(z2_ref[...]), split(z3_ref[...])]
+    for t in range(TILES):
+        value = coefficients[0] * z[0][t] + coefficients[1] * z[1][t] + coefficients[2] * z[2][t]
+        if t < 2:
+            out_ref[:, t * LANES : (t + 1) * LANES] = value[0:EL, :]
+        else:
+            out_ref[:, 2 * LANES : BLK] = value[0:EL, 0 : BLK - 2 * LANES]
+    lane = tile_iota(1)
+    ratio_ref[...] = jnp.where(lane == 0, ratio, jnp.where(good, 1.0, 0.0))
+
+
+def shape(*dims, dtype=jnp.float32):
+    return jax.ShapeDtypeStruct(dims, dtype)
+
+
+def call(kernel, outs, args, scalar_args=()):
+    in_specs = [
+        pl.BlockSpec(memory_space=pltpu.SMEM if n in scalar_args else pltpu.VMEM)
+        for n in range(len(args))
+    ]
+    out_specs = jax.tree.map(lambda _: pl.BlockSpec(memory_space=pltpu.VMEM), outs)
+    return pl.pallas_call(
+        kernel,
+        out_shape=outs,
+        in_specs=in_specs,
+        out_specs=out_specs,
+        compiler_params=pltpu.CompilerParams(vmem_limit_bytes=24 * 2**20),
+    )(*args)
+
+
+def body(rhs, vol_jac, inv_step, face_jac, orientation):
+    nx, ny = lax.axis_size("gx"), lax.axis_size("gy")
+    flat = [(x, y) for x in range(nx) for y in range(ny)]
+
+    def pairs(move):
+        return [(x * ny + y, (move(x, y)[0] % nx) * ny + move(x, y)[1] % ny) for x, y in flat]
+
+    routes = [
+        pairs(lambda x, y: (x ^ 1, y)),
+        pairs(lambda x, y: (x, y ^ 1)),
+        pairs(lambda x, y: (x, y + 1 if y % 2 else y - 1)),
+        pairs(lambda x, y: (x + 1 if x % 2 else x - 1, y)),
+    ]
+
+    def exchange(tx, ty):
+        near_x = lax.ppermute(tx, DEVICES_AXES, routes[0])
+        near_y = lax.ppermute(ty, DEVICES_AXES, routes[1])
+        far_y = lax.ppermute(ty, DEVICES_AXES, routes[2])
+        far_x = lax.ppermute(tx, DEVICES_AXES, routes[3])
+        return near_x, far_x, near_y, far_y
+
+    side = jnp.stack([lax.axis_index("gx") % 2, lax.axis_index("gy") % 2]).astype(jnp.int32)
+    vec, tr = shape(8, WIDE), shape(8, LANES)
+    matrix, diag, g, q, r0, z, tx, ty, tz = call(
+        prepare,
+        (shape(EL, BLK, WIDE), vec, shape(3 * NV, 8, LANES), shape(3, 8, LANES, dtype=jnp.int32), vec, vec, tr, tr, tr),
+        (
+            vol_jac.reshape(EL, BLK, BLK),
+            rhs.reshape(EL, BLK),
+            inv_step.reshape(EL),
+            face_jac.reshape(EL, 6, NV, NV).transpose(2, 3, 0, 1),
+            orientation.reshape(EL, 6),
+        ),
+        scalar_args=(2,),
+    )
+    basis, directions = [r0], [z]
+    for iteration in range(ITERS):
+        around = exchange(tx, ty)
+        part = call(own_part, vec, (matrix, diag, g, q, basis[-1], z, tz))
+        if iteration < ITERS - 1:
+            r, z, tx, ty, tz = call(
+                advance, (vec, vec, tr, tr, tr), (side, part, *around, g, q, matrix, diag), scalar_args=(0,)
+            )
+            basis.append(r)
+            directions.append(z)
+    total = nx * ny
+    sums = call(products, shape(total, LANES), (side, part, *around, g, q, *basis), scalar_args=(0,))
+    sums = lax.all_to_all(sums.reshape(total, 1, LANES), DEVICES_AXES, 0, 0).reshape(total, LANES)
+    update, ratio = call(finish, (shape(EL, BLK), tr), (sums, *directions))
+    fine = ratio[0, 1] > 0.5
+    return lax.cond(
+        fine,
+        lambda: (update.reshape(rhs.shape), ratio[0, 0]),
+        lambda: careful(rhs, vol_jac, inv_step, face_jac, orientation),
+    )
+
+
 def solution(mesh):
     placed = (
         P("gx", "gy", None, None),

time: 1000 us -> 68.2 us (0.07)
  blocking collectives: 758 us -> 0 us
  other arithmetic: 82.4 us -> 0.07 us
  local copies, waits for them, and re-layouts: 68.6 us -> 1.12 us
  matrix products: 52.6 us -> 0 us
  starting transfers between devices: 16.2 us -> 34.9 us
  waiting for transfers between devices: 1.83 us -> 15.7 us
  Pallas kernels: 0 us -> 12.7 us
  between operations: 14.7 us -> 2.6 us
    psum x10 -> x0, blocking collectives: 758 us -> none  [the longest x6 456 us: body(): projection = lax.psum(jnp.sum(image_vec * vector), ('gx', 'gy'))]
    dot_general x32 -> x0, matrix products: 52.6 us -> none  [the longest x3 14.1 us: invert_blocks(): jnp.einsum('...rk,...kc->...rc', element_block, approx, precision=highest)]
    add x2 -> x0, other arithmetic: 50.9 us -> none  [the longest x1 50.3 us: invert_blocks(): element_block = vol_jac + face_block + inv_step[..., None, None] * eye_block]
    add x1 -> x0, local copies, waits for them, and re-layouts: 29.9 us -> none  [invert_blocks(): element_block = vol_jac + face_block + inv_step[..., None, None] * eye_block]
    unnamed x31 -> x8, local copies, waits for them, and re-layouts: 24.4 us -> 0.03 us
    dot_general x1 -> x0, other arithmetic: 18 us -> none  [invert_blocks(): jnp.einsum('...ijn,nm->...injm', node_part, eye_nodes, precision=highest)]
    all_to_all x0 -> x1, waiting for transfers between devices: none -> 12.8 us  [body(): lax.all_to_all(sums.reshape(total, 1, LANES), DEVICES_AXES, 0, 0)]
    pallas_call x0 -> x8, Pallas kernels: none -> 12.7 us  [call(): pl.pallas_call(kernel, out_shape=outs, in_specs=in_specs, out_specs=out_s...]
  transfers between devices with their start and end apart: 12 -> 13, of which waited for: 3 -> 4; matrix products, arithmetic and copies ran while one was open for 1% -> 0% of each run, Pallas kernels for 0% -> 2%
where the time goes in v1:
time: 68.2 us; the launch traced here: 68 us
  starting transfers between devices  34.9 us (51%)
  waiting for transfers between devices  15.7 us (23%)
  Pallas kernels  12.7 us (19%)
  between operations  2.6 us (4%)
  local copies, waits for them, and re-layouts  1.12 us (2%)
  loops' own time  0.88 us (1%)
    ppermute x3, starting transfers between devices, exchange(): near_x = lax.ppermute(tx, DEVICES_AXES, routes[0])  13.5 us
    all_to_all x1, waiting for transfers between devices, body(): lax.all_to_all(sums.reshape(total, 1, LANES), DEVICES_AXES, 0, 0)  12.8 us
    pallas_call x8, Pallas kernels, call(): pl.pallas_call(kernel, out_shape=outs, in_specs=in_specs, out_specs=out_s...  12.7 us
    ppermute x3, starting transfers between devices, exchange(): far_y = lax.ppermute(ty, DEVICES_AXES, routes[2])  9.91 us
    all_to_all x1, starting transfers between devices, body(): lax.all_to_all(sums.reshape(total, 1, LANES), DEVICES_AXES, 0, 0)  9.71 us
    ppermute x3, waiting for transfers between devices, exchange(): far_y = lax.ppermute(ty, DEVICES_AXES, routes[2])  2.92 us
    ppermute x3, starting transfers between devices, exchange(): near_y = lax.ppermute(ty, DEVICES_AXES, routes[1])  1.41 us
  transfers between devices with their start and end apart: 13, of which 4 were waited for; matrix products, arithmetic and copies ran while one was open for 0% of the time, Pallas kernels for 2%

profile of v1, /device:TPU:1, one launch (start us, length us, event | category | flops | bytes accessed | tf_op | source)
XLA Modules:
  0.0 68.0 jit_solution(3350279153108562563)
XLA Ops:
  0.6 4.2 %shard_map.92 = (f32[4,320,384]{2,1,0:T(8,128)S(1)}, f32[8,384]{1,0:T(8,128)S(1)}, f32[15,8,128]{2,1,0:T(8,128)S(1)}, s32[3,8,128]{2,1,0:T(8,128)S(1)}, f32[8,38...) custom-call(f32[4,320,320]{2,1,0:T(8,128)} %bitcast.248, ...), custom_call_target="tpu_custom_call" | custom-call | tf_op jit(solution)/shard_map/pallas_call | solution.py:545
  4.9 3.3 %collective-permute-start.12 = (f32[8,128]{1,0:T(8,128)S(1)}, f32[8,128]{1,0:T(8,128)S(1)}, u32[]{:S(2)}, u32[]{:S(2)}) collective-permute-start(f32[8,128]{1,0:T(8,128)S(1)} %get-tuple-element.56), channel_id=1, source_target_pairs={{0,8},{1,9},{2,10},{3,11},{4,12},{5,13},{6,14},{7,15},{8,0},{9,1},... | collective-permute-start | bytes 12296 | tf_op jit(solution)/shard_map/ppermute | solution.py:569
  8.2 1.1 %collective-permute-start.14 = (f32[8,128]{1,0:T(8,128)S(1)}, f32[8,128]{1,0:T(8,128)S(1)}, u32[]{:S(2)}, u32[]{:S(2)}) collective-permute-start(f32[8,128]{1,0:T(8,128)S(1)} %get-tuple-element.57), channel_id=1, source_target_pairs={{0,1},{1,0},{2,3},{3,2},{4,5},{5,4},{6,7},{7,6},{8,9},{9,8},{10,11... | collective-permute-start | bytes 12296 | tf_op jit(solution)/shard_map/ppermute | solution.py:570
  9.3 2.7 %collective-permute-start.15 = (f32[8,128]{1,0:T(8,128)S(1)}, f32[8,128]{1,0:T(8,128)S(1)}, u32[]{:S(2)}, u32[]{:S(2)}) collective-permute-start(f32[8,128]{1,0:T(8,128)S(1)} %get-tuple-element.57), channel_id=1, source_target_pairs={{0,7},{1,2},{2,1},{3,4},{4,3},{5,6},{6,5},{7,0},{8,15},{9,10},{10,... | collective-permute-start | bytes 12296 | tf_op jit(solution)/shard_map/ppermute | solution.py:571
  12.1 0.4 shard_map.93.part_ref
  12.5 1.4 %collective-permute-done.15.ry_ref = f32[8,128]{1,0:T(8,128)S(1)} collective-permute-done((f32[8,128]{1,0:T(8,128)S(1)}, f32[8,128]{1,0:T(8,128)S(1)}, u32[]{:S(2)}, u32[]{:S(2)}) %collective-permute-start.15) | collective-permute-done | bytes 4128 | tf_op jit(solution)/shard_map/ppermute | solution.py:571
  13.9 2.6 %shard_map.94 = (f32[8,384]{1,0:T(8,128)S(1)}, f32[8,384]{1,0:T(8,128)S(1)}, f32[8,128]{1,0:T(8,128)S(1)}, f32[8,128]{1,0:T(8,128)S(1)}, f32[8,128]{1,0:T(8,128)S(1)}) custom-call(s32[2]{0:T(128)S(1)} %pad_add_fusion.side_ref, f32[8,384]{1,0:T(8,128)S(1)} %shard_map.93.part_ref, f32[8,128]{1,0:T(8,128)S(1)} %collective-permute-done.12.rc_ref, ...), custom_call_target="tpu_custom_call" | custom-call | tf_op jit(solution)/shard_map/pallas_call | solution.py:545
  16.5 7.4 %collective-permute-start.16 = (f32[8,128]{1,0:T(8,128)S(1)}, f32[8,128]{1,0:T(8,128)S(1)}, u32[]{:S(2)}, u32[]{:S(2)}) collective-permute-start(f32[8,128]{1,0:T(8,128)S(1)} %get-tuple-element.61), channel_id=1, source_target_pairs={{0,8},{1,9},{2,10},{3,11},{4,12},{5,13},{6,14},{7,15},{8,0},{9,1},... | collective-permute-start | bytes 12296 | tf_op jit(solution)/shard_map/ppermute | solution.py:569
  23.8 3.6 %collective-permute-start.19 = (f32[8,128]{1,0:T(8,128)S(1)}, f32[8,128]{1,0:T(8,128)S(1)}, u32[]{:S(2)}, u32[]{:S(2)}) collective-permute-start(f32[8,128]{1,0:T(8,128)S(1)} %get-tuple-element.62), channel_id=1, source_target_pairs={{0,7},{1,2},{2,1},{3,4},{4,3},{5,6},{6,5},{7,0},{8,15},{9,10},{10,... | collective-permute-start | bytes 12296 | tf_op jit(solution)/shard_map/ppermute | solution.py:571
  27.4 0.4 shard_map.95.part_ref
  27.9 0.6 collective-permute-done.19.ry_ref
  28.5 2.6 %shard_map.96 = (f32[8,384]{1,0:T(8,128)S(1)}, f32[8,384]{1,0:T(8,128)S(1)}, f32[8,128]{1,0:T(8,128)S(1)}, f32[8,128]{1,0:T(8,128)S(1)}, f32[8,128]{1,0:T(8,128)S(1)}) custom-call(s32[2]{0:T(128)S(1)} %pad_add_fusion.side_ref, f32[8,384]{1,0:T(8,128)S(1)} %shard_map.95.part_ref, f32[8,128]{1,0:T(8,128)S(1)} %collective-permute-done.16.rc_ref, ...), custom_call_target="tpu_custom_call" | custom-call | tf_op jit(solution)/shard_map/pallas_call | solution.py:545
  31.1 2.8 %collective-permute-start.20 = (f32[8,128]{1,0:T(8,128)S(1)}, f32[8,128]{1,0:T(8,128)S(1)}, u32[]{:S(2)}, u32[]{:S(2)}) collective-permute-start(f32[8,128]{1,0:T(8,128)S(1)} %get-tuple-element.66), channel_id=1, source_target_pairs={{0,8},{1,9},{2,10},{3,11},{4,12},{5,13},{6,14},{7,15},{8,0},{9,1},... | collective-permute-start | bytes 12296 | tf_op jit(solution)/shard_map/ppermute | solution.py:569
  33.9 0.3 collective-permute-start.21
  34.6 3.6 %collective-permute-start.23 = (f32[8,128]{1,0:T(8,128)S(1)}, f32[8,128]{1,0:T(8,128)S(1)}, u32[]{:S(2)}, u32[]{:S(2)}) collective-permute-start(f32[8,128]{1,0:T(8,128)S(1)} %get-tuple-element.67), channel_id=1, source_target_pairs={{0,7},{1,2},{2,1},{3,4},{4,3},{5,6},{6,5},{7,0},{8,15},{9,10},{10,... | collective-permute-start | bytes 12296 | tf_op jit(solution)/shard_map/ppermute | solution.py:571
  38.2 0.4 shard_map.97.part_ref
  38.6 0.9 %collective-permute-done.23.ry_ref = f32[8,128]{1,0:T(8,128)S(1)} collective-permute-done((f32[8,128]{1,0:T(8,128)S(1)}, f32[8,128]{1,0:T(8,128)S(1)}, u32[]{:S(2)}, u32[]{:S(2)}) %collective-permute-start.23) | collective-permute-done | bytes 4128 | tf_op jit(solution)/shard_map/ppermute | solution.py:571
  39.5 1.5 %shard_map.98 = f32[256,128]{1,0:T(8,128)} custom-call(s32[2]{0:T(128)S(1)} %pad_add_fusion.side_ref, f32[8,384]{1,0:T(8,128)S(1)} %shard_map.97.part_ref, f32[8,128]{1,0:T(8,128)S(1)} %collective-permute-done.20.rc_ref, f32[8,128]{1,0:T(8,128)S(1)} %collective-permute-done.21.rz_ref, f32[8,128]{1,0:T(8,128)S(1)} %collective-permute-done.22.rx_ref, ...), custom_call_target="tpu_custom_call" | custom-call | tf_op jit(solution)/shard_map/pallas_call | solution.py:545
  40.9 9.7 %all-to-all-start = ((f32[256,1,128]{2,1,0:T(1,128)}), f32[256,1,128]{2,1,0:T(1,128)S(1)}, u32[]{:S(2)}, u32[]{:S(2)}) async-start(f32[256,1,128]{2,1,0:T(1,128)} %bitcast.86), calls=%async_computation | async-start | bytes 262144 | tf_op jit(solution)/shard_map/all_to_all | solution.py:601
  50.7 12.8 %all-to-all-done = f32[256,1,128]{2,1,0:T(1,128)S(1)} async-done(((f32[256,1,128]{2,1,0:T(1,128)}), f32[256,1,128]{2,1,0:T(1,128)S(1)}, u32[]{:S(2)}, u32[]{:S(2)}) %all-to-all-start) | async-done | bytes 131104 | tf_op jit(solution)/shard_map/all_to_all | solution.py:601
  63.4 0.8 %shard_map.99 = (f32[4,320]{1,0:T(4,128)}, f32[8,128]{1,0:T(8,128)S(1)}) custom-call(f32[256,128]{1,0:T(8,128)S(1)} %bitcast.246, f32[8,384]{1,0:T(8,128)S(1)} %get-tuple-element.54.z_ref.z1_ref, f32[8,384]{1,0:T(8,128)S(1)} %get-tuple-element.59.z_ref.z2_ref, f32[8,384]{1,0:T(8,128)S(1)} %get-tuple-element.64.z_ref.z3_ref), custom_call_target="tpu_custom_call" | custom-call | tf_op jit(solution)/shard_map/pallas_call | solution.py:545
  64.2 0.6 slice.100
  65.5 1.4 %conditional.1 = (f32[1,1,4,320]{3,2,1,0:T(4,128)}, f32[]{:T(128)}) conditional(s32[]{:T(128)} %bitcast.88, (f32[1,1,4]{2,1,0:T(1,128)S(1)}, (), f32[1,1,4,6,5,5]{3,2,5,4,1,0:T(4,128)S(1)}, f32[1,1,4,320,320]{4,3,2,1,0:T(8,128)}, f32[1,1,4,320]{3,2,1,0:T(4,128)S(1)}, /*index=5*/s32[1,1,4,6]{3,2,1,0:T(4,128)S(1)}, ()) %tuple.51, ...), branch_computations={%region_0.22_spmd, %region_22.23_spmd} | conditional | flops 9523977216 | bytes 68001136 | solution.py:604
  65.7 0.5 slice.98
  (22 shorter events, 0.4 us)
Async XLA Ops:
  4.9 7.6 %collective-permute-start.12 = (f32[8,128]{1,0:T(8,128)S(1)}, f32[8,128]{1,0:T(8,128)S(1)}, u32[]{:S(2)}, u32[]{:S(2)}) collective-permute-start(f32[8,128]{1,0:T(8,128)S(1)} %get-tuple-element.56), channel_id=1, source_target_pairs={{0,8},{1,9},{2,10},{3,11},{4,12},{5,13},{6,14},{7,15},{8,0},{9,1},... | collective-permute-start | bytes 12296 | tf_op jit(solution)/shard_map/ppermute | solution.py:569
  8.2 4.3 %collective-permute-start.13 = (f32[8,128]{1,0:T(8,128)S(1)}, f32[8,128]{1,0:T(8,128)S(1)}, u32[]{:S(2)}, u32[]{:S(2)}) collective-permute-start(f32[8,128]{1,0:T(8,128)S(1)} %get-tuple-element.56), channel_id=1, source_target_pairs={{0,248},{1,249},{2,250},{3,251},{4,252},{5,253},{6,254},{7,255},{8... | collective-permute-start | bytes 12296 | tf_op jit(solution)/shard_map/ppermute | solution.py:572
  8.2 4.3 %collective-permute-start.14 = (f32[8,128]{1,0:T(8,128)S(1)}, f32[8,128]{1,0:T(8,128)S(1)}, u32[]{:S(2)}, u32[]{:S(2)}) collective-permute-start(f32[8,128]{1,0:T(8,128)S(1)} %get-tuple-element.57), channel_id=1, source_target_pairs={{0,1},{1,0},{2,3},{3,2},{4,5},{5,4},{6,7},{7,6},{8,9},{9,8},{10,11... | collective-permute-start | bytes 12296 | tf_op jit(solution)/shard_map/ppermute | solution.py:570
  9.3 4.6 %collective-permute-start.15 = (f32[8,128]{1,0:T(8,128)S(1)}, f32[8,128]{1,0:T(8,128)S(1)}, u32[]{:S(2)}, u32[]{:S(2)}) collective-permute-start(f32[8,128]{1,0:T(8,128)S(1)} %get-tuple-element.57), channel_id=1, source_target_pairs={{0,7},{1,2},{2,1},{3,4},{4,3},{5,6},{6,5},{7,0},{8,15},{9,10},{10,... | collective-permute-start | bytes 12296 | tf_op jit(solution)/shard_map/ppermute | solution.py:571
  16.5 11.4 %collective-permute-start.16 = (f32[8,128]{1,0:T(8,128)S(1)}, f32[8,128]{1,0:T(8,128)S(1)}, u32[]{:S(2)}, u32[]{:S(2)}) collective-permute-start(f32[8,128]{1,0:T(8,128)S(1)} %get-tuple-element.61), channel_id=1, source_target_pairs={{0,8},{1,9},{2,10},{3,11},{4,12},{5,13},{6,14},{7,15},{8,0},{9,1},... | collective-permute-start | bytes 12296 | tf_op jit(solution)/shard_map/ppermute | solution.py:569
  23.8 4.0 %collective-permute-start.17 = (f32[8,128]{1,0:T(8,128)S(1)}, f32[8,128]{1,0:T(8,128)S(1)}, u32[]{:S(2)}, u32[]{:S(2)}) collective-permute-start(f32[8,128]{1,0:T(8,128)S(1)} %get-tuple-element.61), channel_id=1, source_target_pairs={{0,248},{1,249},{2,250},{3,251},{4,252},{5,253},{6,254},{7,255},{8... | collective-permute-start | bytes 12296 | tf_op jit(solution)/shard_map/ppermute | solution.py:572
  23.8 4.0 %collective-permute-start.18 = (f32[8,128]{1,0:T(8,128)S(1)}, f32[8,128]{1,0:T(8,128)S(1)}, u32[]{:S(2)}, u32[]{:S(2)}) collective-permute-start(f32[8,128]{1,0:T(8,128)S(1)} %get-tuple-element.62), channel_id=1, source_target_pairs={{0,1},{1,0},{2,3},{3,2},{4,5},{5,4},{6,7},{7,6},{8,9},{9,8},{10,11... | collective-permute-start | bytes 12296 | tf_op jit(solution)/shard_map/ppermute | solution.py:570
  23.8 4.6 %collective-permute-start.19 = (f32[8,128]{1,0:T(8,128)S(1)}, f32[8,128]{1,0:T(8,128)S(1)}, u32[]{:S(2)}, u32[]{:S(2)}) collective-permute-start(f32[8,128]{1,0:T(8,128)S(1)} %get-tuple-element.62), channel_id=1, source_target_pairs={{0,7},{1,2},{2,1},{3,4},{4,3},{5,6},{6,5},{7,0},{8,15},{9,10},{10,... | collective-permute-start | bytes 12296 | tf_op jit(solution)/shard_map/ppermute | solution.py:571
  27.8 37.7 %copy-start.2 = (f32[1,1,4,320]{3,2,1,0:T(4,128)S(1)}, f32[1,1,4,320]{3,2,1,0:T(4,128)}, u32[]{:S(2)}) copy-start(f32[1,1,4,320]{3,2,1,0:T(4,128)} %param.9) | copy-start | bytes 15364
  27.8 37.6 %copy-start.6 = (f32[1,1,4,6,5,5]{3,2,5,4,1,0:T(4,128)S(1)}, f32[1,1,4,6,5,5]{3,2,5,4,1,0:T(4,128)}, u32[]{:S(2)}) copy-start(f32[1,1,4,6,5,5]{3,2,5,4,1,0:T(4,128)} %param.12) | copy-start | bytes 7204
  27.8 37.6 %copy-start.8 = (f32[1,1,4]{2,1,0:T(1,128)S(1)}, f32[1,1,4]{2,1,0:T(1,128)}, u32[]{:S(2)}) copy-start(f32[1,1,4]{2,1,0:T(1,128)} %param.11) | copy-start | bytes 52
  27.8 37.6 %copy-start.9 = (s32[1,1,4,6]{3,2,1,0:T(4,128)S(1)}, s32[1,1,4,6]{3,2,1,0:T(4,128)}, u32[]{:S(2)}) copy-start(s32[1,1,4,6]{3,2,1,0:T(4,128)} %param.13) | copy-start | bytes 292
  31.1 7.5 %collective-permute-start.20 = (f32[8,128]{1,0:T(8,128)S(1)}, f32[8,128]{1,0:T(8,128)S(1)}, u32[]{:S(2)}, u32[]{:S(2)}) collective-permute-start(f32[8,128]{1,0:T(8,128)S(1)} %get-tuple-element.66), channel_id=1, source_target_pairs={{0,8},{1,9},{2,10},{3,11},{4,12},{5,13},{6,14},{7,15},{8,0},{9,1},... | collective-permute-start | bytes 12296 | tf_op jit(solution)/shard_map/ppermute | solution.py:569
  33.9 4.6 %collective-permute-start.21 = (f32[8,128]{1,0:T(8,128)S(1)}, f32[8,128]{1,0:T(8,128)S(1)}, u32[]{:S(2)}, u32[]{:S(2)}) collective-permute-start(f32[8,128]{1,0:T(8,128)S(1)} %get-tuple-element.66), channel_id=1, source_target_pairs={{0,248},{1,249},{2,250},{3,251},{4,252},{5,253},{6,254},{7,255},{8... | collective-permute-start | bytes 12296 | tf_op jit(solution)/shard_map/ppermute | solution.py:572
  34.2 4.3 %collective-permute-start.22 = (f32[8,128]{1,0:T(8,128)S(1)}, f32[8,128]{1,0:T(8,128)S(1)}, u32[]{:S(2)}, u32[]{:S(2)}) collective-permute-start(f32[8,128]{1,0:T(8,128)S(1)} %get-tuple-element.67), channel_id=1, source_target_pairs={{0,1},{1,0},{2,3},{3,2},{4,5},{5,4},{6,7},{7,6},{8,9},{9,8},{10,11... | collective-permute-start | bytes 12296 | tf_op jit(solution)/shard_map/ppermute | solution.py:570
  34.6 4.9 %collective-permute-start.23 = (f32[8,128]{1,0:T(8,128)S(1)}, f32[8,128]{1,0:T(8,128)S(1)}, u32[]{:S(2)}, u32[]{:S(2)}) collective-permute-start(f32[8,128]{1,0:T(8,128)S(1)} %get-tuple-element.67), channel_id=1, source_target_pairs={{0,7},{1,2},{2,1},{3,4},{4,3},{5,6},{6,5},{7,0},{8,15},{9,10},{10,... | collective-permute-start | bytes 12296 | tf_op jit(solution)/shard_map/ppermute | solution.py:571
  40.9 22.5 %all-to-all-start = ((f32[256,1,128]{2,1,0:T(1,128)}), f32[256,1,128]{2,1,0:T(1,128)S(1)}, u32[]{:S(2)}, u32[]{:S(2)}) async-start(f32[256,1,128]{2,1,0:T(1,128)} %bitcast.86), calls=%async_computation | async-start | bytes 262144 | tf_op jit(solution)/shard_map/all_to_all | solution.py:601

commit v2 on v1

--- a/solution.py
+++ b/solution.py
@@ -206,6 +206,7 @@
 MIN_SCALE = 1e-18
 MAX_SCALE = 1e30
 DEVICES_AXES = ("gx", "gy")
+ROUTE_ORDER = ("far x", "far y", "near y", "near x")
 
 
 def tile_iota(dim):
@@ -245,7 +246,7 @@
     return [offset == 8 * k for k in range(LANES // 8)]
 
 
-def couple_rows(f_ref, y):
+def couple_rows(h_ref, y):
     masks = row_masks()
     tiles = [[] for _ in range(TILES)]
     for e in range(EL):
@@ -253,9 +254,9 @@
         acc = [jnp.zeros((8, LANES), jnp.float32) for _ in range(TILES)]
         for g in range(GROUPS):
             rows = slice(8 * g, 8 * g + 8)
-            p = f_ref[e, rows, 0:LANES] * spread[0]
-            p = p + f_ref[e, rows, LANES : 2 * LANES] * spread[1]
-            p = p + f_ref[e, rows, 2 * LANES : WIDE] * spread[2]
+            p = h_ref[e, rows, 0:LANES] * spread[0]
+            p = p + h_ref[e, rows, LANES : 2 * LANES] * spread[1]
+            p = p + h_ref[e, rows, 2 * LANES : WIDE] * spread[2]
             total = jnp.sum(p, axis=1, keepdims=True)
             t, k = divmod(g, LANES // 8)
             acc[t] = jnp.where(masks[k], total, acc[t])
@@ -264,13 +265,33 @@
     return [collect(parts) for parts in tiles]
 
 
-def series(f_ref, start, inverse):
+def couple_twice(h_ref, t_ref, y):
+    tiles = [[] for _ in range(TILES)]
+    for e in range(EL):
+        spread = [jnp.broadcast_to(part[e : e + 1, :], (8, LANES)) for part in y]
+        acc = [jnp.zeros((8, LANES), jnp.float32) for _ in range(TILES)]
+        for g in range(GROUPS):
+            rows = slice(8 * g, 8 * g + 8)
+            p = h_ref[e, rows, 0:LANES] * spread[0]
+            p = p + h_ref[e, rows, LANES : 2 * LANES] * spread[1]
+            p = p + h_ref[e, rows, 2 * LANES : WIDE] * spread[2]
+            total = jnp.sum(p, axis=1, keepdims=True)
+            for t in range(TILES):
+                acc[t] = acc[t] + t_ref[e, rows, t * LANES : (t + 1) * LANES] * total
+        for t in range(TILES):
+            tiles[t].append(acc[t])
+    return [collect(parts) for parts in tiles]
+
+
+def series(h_ref, t_ref, start):
+    moved = couple_rows(h_ref, start)
+    first = tuple(start[t] + moved[t] for t in range(TILES))
+
     def step(_, y):
-        moved = couple_rows(f_ref, y)
-        return tuple(inverse[t] * (start[t] + moved[t]) for t in range(TILES))
-
-    first = tuple(inverse[t] * start[t] for t in range(TILES))
-    return list(lax.fori_loop(0, 2**NS_STEPS - 1, step, first))
+        moved = couple_twice(h_ref, t_ref, y)
+        return tuple(first[t] + moved[t] for t in range(TILES))
+
+    return list(lax.fori_loop(0, 2 ** (NS_STEPS - 1) - 1, step, first))
 
 
 def traces_of(z):
@@ -347,7 +368,11 @@
         ref[:, t * LANES : (t + 1) * LANES] = parts[t]
 
 
-def prepare(vol_ref, rhs_ref, inv_ref, fj_ref, ori_ref, f_ref, d_ref, g_ref, q_ref, r_ref, z_ref, tx_ref, ty_ref, tz_ref):
+def prepare(vol_ref, rhs_ref, inv_ref, fj_ref, ori_ref, m_ref, d_ref, g_ref, q_ref, r_ref, w_ref, z_ref, tx_ref, ty_ref, tz_ref, held_ref, sems):
+    h_ref, t_ref = m_ref.at[0], m_ref.at[1]
+    copies = [pltpu.make_async_copy(vol_ref.at[e], held_ref.at[e], sems.at[e]) for e in range(EL)]
+    for copy in copies:
+        copy.start()
     row, lane = tile_iota(0), tile_iota(1)
     zero = jnp.zeros((8, LANES), jnp.float32)
     r_ref[...] = jnp.zeros((8, WIDE), jnp.float32)
@@ -400,79 +425,101 @@
                 value = jnp.where(lane < NP, value, 0.0)
             tiles.append(value)
         node_part.append(tiles)
-    shifts = zero
-    for e in range(EL):
-        shifts = jnp.where((row & 3) == e, inv_ref[e], shifts)
     masks = row_masks()
     node_offset = node - row
-    diag_tiles = [[] for _ in range(TILES)]
+    inverse = [zero] * TILES
     for e in range(EL):
-        acc = [zero for _ in range(TILES)]
+        copies[e].wait()
+
+        def volume(g, t):
+            rows = slice(8 * g, 8 * g + 8)
+            if t < 2:
+                return held_ref[e, rows, t * LANES : (t + 1) * LANES]
+            return jnp.concatenate([held_ref[e, rows, 2 * LANES : BLK], jnp.zeros((8, WIDE - BLK), jnp.float32)], axis=1)
+
+        diag = [zero] * TILES
+        for g in range(GROUPS):
+            t, k = divmod(g, LANES // 8)
+            diag[t] = jnp.where(masks[k], volume(g, t), diag[t])
+        scale = []
+        for t in range(TILES):
+            total = diag[t]
+            for step in (4, 2, 1):
+                total = total + turn(total, step)
+            low, high = node_part[2 * t][t][e : e + 1, :], node_part[min(2 * t + 1, NV - 1)][t][e : e + 1, :]
+            own_row = jnp.where(lane[0:1] < NP, low, high) if t < 2 else low
+            total = total + jnp.broadcast_to(own_row, (8, LANES)) + inv_ref[e]
+            if t == 2:
+                total = jnp.where(lane < NP, total, 1.0)
+            scale.append(1.0 / total)
+            inverse[t] = jnp.where((row & 3) == e, scale[t], inverse[t])
         for i in range(NV):
             spread = [jnp.broadcast_to(node_part[i][t][e : e + 1, :], (8, LANES)) for t in range(TILES)]
             for gi in range(NP // 8):
                 g = i * (NP // 8) + gi
-                rows = slice(8 * g, 8 * g + 8)
                 td, k = divmod(g, LANES // 8)
                 same_node = node_offset == 8 * gi
                 for t in range(TILES):
-                    if t < 2:
-                        vol = vol_ref[e, rows, t * LANES : (t + 1) * LANES]
-                        value = -vol - jnp.where(same_node, spread[t], 0.0)
-                        if t == td:
-                            acc[t] = jnp.where(masks[k], value, acc[t])
-                            value = jnp.where(masks[k], 0.0, value)
-                        f_ref[e, rows, t * LANES : (t + 1) * LANES] = value
-                    else:
-                        value = jnp.concatenate([vol_ref[e, rows, 2 * LANES : BLK], jnp.zeros((8, WIDE - BLK), jnp.float32)], axis=1)
-                        value = -value - jnp.where(same_node, spread[t], 0.0)
-                        if t == td:
-                            acc[t] = jnp.where(masks[k], value, acc[t])
-                            value = jnp.where(masks[k], 0.0, value)
-                        f_ref[e, rows, 2 * LANES : WIDE] = value
-        for t in range(TILES):
-            diag_tiles[t].append(acc[t])
-    diag = [shifts - collect(parts) for parts in diag_tiles]
-    diag[2] = jnp.where(lane < NP, diag[2], 1.0)
-    put(d_ref, diag)
-    z = series(f_ref, start, [1.0 / x for x in diag])
+                    value = volume(g, t) + jnp.where(same_node, spread[t], 0.0)
+                    value = -(value * scale[t])
+                    if t == td:
+                        value = jnp.where(masks[k], 0.0, value)
+                    h_ref[e, 8 * g : 8 * g + 8, t * LANES : (t + 1) * LANES] = value
+        for bi in range(TILES):
+            size = min(LANES, BLK - bi * LANES)
+            for bj in range(TILES):
+                part = h_ref[e, bi * LANES : bi * LANES + size, bj * LANES : (bj + 1) * LANES]
+                if size < LANES:
+                    part = jnp.concatenate([part, jnp.zeros((LANES - size, LANES), jnp.float32)], axis=0)
+                count = min(LANES, BLK - bj * LANES)
+                t_ref[e, bj * LANES : bj * LANES + count, bi * LANES : (bi + 1) * LANES] = part.T[0:count, :]
+    put(d_ref, inverse)
+    w = series(h_ref, t_ref, start)
+    put(w_ref, w)
+    z = [inverse[t] * w[t] for t in range(TILES)]
     put(z_ref, z)
     tx_ref[...], ty_ref[...], tz_ref[...] = traces_of(z)
 
 
-def own_part(f_ref, d_ref, g_ref, q_ref, r_ref, z_ref, tz_ref, out_ref):
-    r, z, diag = split(r_ref[...]), split(z_ref[...]), split(d_ref[...])
-    moved = couple_rows(f_ref, z)
+def own_part(m_ref, g_ref, q_ref, r_ref, w_ref, tz_ref, out_ref):
+    r, w = split(r_ref[...]), split(w_ref[...])
+    moved = couple_rows(m_ref.at[0], w)
     third = fold(through_faces(2, across_third(tz_ref[...]), g_ref, q_ref))
-    put(out_ref, [diag[t] * z[t] - moved[t] - r[t] + third[t] for t in range(TILES)])
-
-
-def arrived(side_ref, own_axis, pair_ref, far_ref):
-    odd = side_ref[own_axis] == 1
+    put(out_ref, [w[t] - moved[t] - r[t] + third[t] for t in range(TILES)])
+
+
+def arrived(own_axis, pair_ref, far_ref):
+    odd = lax.rem(lax.axis_index(own_axis), 2) == 1
     near, far = pair_ref[...], far_ref[...]
     before = jnp.where(odd, near, far)
     after = jnp.where(odd, far, near)
     return turn(jnp.where(tile_iota(0) >= 4, before, after), 4)
 
 
-def next_vector(side_ref, part_ref, c_ref, z_ref, x_ref, y_ref, g_ref, q_ref):
-    first = through_faces(0, arrived(side_ref, 0, c_ref, z_ref), g_ref, q_ref)
-    second = through_faces(1, arrived(side_ref, 1, x_ref, y_ref), g_ref, q_ref)
+def by_route(*refs):
+    return [refs[ROUTE_ORDER.index(name)] for name in ("near x", "far x", "near y", "far y")]
+
+
+def next_vector(part_ref, c_ref, z_ref, x_ref, y_ref, g_ref, q_ref):
+    first = through_faces(0, arrived("gx", c_ref, z_ref), g_ref, q_ref)
+    second = through_faces(1, arrived("gy", x_ref, y_ref), g_ref, q_ref)
     lifted = fold([first[t] + second[t] for t in range(TILES)])
     part = split(part_ref[...])
     return [part[t] + lifted[t] for t in range(TILES)]
 
 
-def advance(side_ref, part_ref, rc_ref, rz_ref, rx_ref, ry_ref, g_ref, q_ref, f_ref, d_ref, r_ref, z_ref, tx_ref, ty_ref, tz_ref):
-    r = next_vector(side_ref, part_ref, rc_ref, rz_ref, rx_ref, ry_ref, g_ref, q_ref)
+def advance(part_ref, a0_ref, a1_ref, a2_ref, a3_ref, g_ref, q_ref, m_ref, d_ref, r_ref, w_ref, z_ref, tx_ref, ty_ref, tz_ref):
+    r = next_vector(part_ref, *by_route(a0_ref, a1_ref, a2_ref, a3_ref), g_ref, q_ref)
     put(r_ref, r)
-    z = series(f_ref, r, [1.0 / x for x in split(d_ref[...])])
+    w = series(m_ref.at[0], m_ref.at[1], r)
+    put(w_ref, w)
+    z = [a * b for a, b in zip(split(d_ref[...]), w)]
     put(z_ref, z)
     tx_ref[...], ty_ref[...], tz_ref[...] = traces_of(z)
 
 
-def products(side_ref, part_ref, rc_ref, rz_ref, rx_ref, ry_ref, g_ref, q_ref, r0_ref, r1_ref, r2_ref, out_ref):
-    last = next_vector(side_ref, part_ref, rc_ref, rz_ref, rx_ref, ry_ref, g_ref, q_ref)
+def products(part_ref, a0_ref, a1_ref, a2_ref, a3_ref, g_ref, q_ref, r0_ref, r1_ref, r2_ref, out_ref):
+    last = next_vector(part_ref, *by_route(a0_ref, a1_ref, a2_ref, a3_ref), g_ref, q_ref)
     basis = [split(r0_ref[...]), split(r1_ref[...]), split(r2_ref[...]), last]
     lane = tile_iota(1)
     acc = jnp.zeros((8, LANES), jnp.float32)
@@ -484,11 +531,10 @@
             slot += 1
     for step in (1, 2):
         acc = acc + turn(acc, step)
-    for n in range(out_ref.shape[0] // 8):
-        out_ref[8 * n : 8 * n + 8, :] = acc
-
-
-def finish(sums_ref, z1_ref, z2_ref, z3_ref, out_ref, ratio_ref):
+    out_ref[...] = acc
+
+
+def finish(sums_ref, z1_ref, z2_ref, z3_ref, out_ref, ratio_ref, fine_ref):
     acc = jnp.zeros((8, LANES), jnp.float32)
     parts = [acc] * 4
     for n in range(sums_ref.shape[0] // 8):
@@ -528,26 +574,31 @@
             out_ref[:, t * LANES : (t + 1) * LANES] = value[0:EL, :]
         else:
             out_ref[:, 2 * LANES : BLK] = value[0:EL, 0 : BLK - 2 * LANES]
-    lane = tile_iota(1)
-    ratio_ref[...] = jnp.where(lane == 0, ratio, jnp.where(good, 1.0, 0.0))
+    ratio_ref[0] = ratio[0, 0]
+    fine_ref[0] = jnp.where(good, 1, 0)[0, 0]
 
 
 def shape(*dims, dtype=jnp.float32):
     return jax.ShapeDtypeStruct(dims, dtype)
 
 
-def call(kernel, outs, args, scalar_args=()):
+def call(kernel, outs, args, scalar_args=(), scalar_outs=(), far_args=(), scratch=()):
     in_specs = [
-        pl.BlockSpec(memory_space=pltpu.SMEM if n in scalar_args else pltpu.VMEM)
+        pl.BlockSpec(memory_space=pltpu.SMEM if n in scalar_args else pl.ANY if n in far_args else pltpu.VMEM)
         for n in range(len(args))
     ]
-    out_specs = jax.tree.map(lambda _: pl.BlockSpec(memory_space=pltpu.VMEM), outs)
+    single = not isinstance(outs, tuple)
+    out_specs = [
+        pl.BlockSpec(memory_space=pltpu.SMEM if n in scalar_outs else pltpu.VMEM)
+        for n in range(1 if single else len(outs))
+    ]
     return pl.pallas_call(
         kernel,
         out_shape=outs,
         in_specs=in_specs,
-        out_specs=out_specs,
-        compiler_params=pltpu.CompilerParams(vmem_limit_bytes=24 * 2**20),
+        out_specs=out_specs[0] if single else tuple(out_specs),
+        scratch_shapes=scratch,
+        compiler_params=pltpu.CompilerParams(vmem_limit_bytes=16 * 2**20),
     )(*args)
 
 
@@ -558,25 +609,29 @@
     def pairs(move):
         return [(x * ny + y, (move(x, y)[0] % nx) * ny + move(x, y)[1] % ny) for x, y in flat]
 
-    routes = [
-        pairs(lambda x, y: (x ^ 1, y)),
-        pairs(lambda x, y: (x, y ^ 1)),
-        pairs(lambda x, y: (x, y + 1 if y % 2 else y - 1)),
-        pairs(lambda x, y: (x + 1 if x % 2 else x - 1, y)),
-    ]
+    routes = {
+        "near x": pairs(lambda x, y: (x ^ 1, y)),
+        "far x": pairs(lambda x, y: (x + 1 if x % 2 else x - 1, y)),
+        "near y": pairs(lambda x, y: (x, y ^ 1)),
+        "far y": pairs(lambda x, y: (x, y + 1 if y % 2 else y - 1)),
+    }
 
     def exchange(tx, ty):
-        near_x = lax.ppermute(tx, DEVICES_AXES, routes[0])
-        near_y = lax.ppermute(ty, DEVICES_AXES, routes[1])
-        far_y = lax.ppermute(ty, DEVICES_AXES, routes[2])
-        far_x = lax.ppermute(tx, DEVICES_AXES, routes[3])
-        return near_x, far_x, near_y, far_y
-
-    side = jnp.stack([lax.axis_index("gx") % 2, lax.axis_index("gy") % 2]).astype(jnp.int32)
+        return [
+            lax.ppermute(tx if name.endswith("x") else ty, DEVICES_AXES, routes[name]) for name in ROUTE_ORDER
+        ]
+
     vec, tr = shape(8, WIDE), shape(8, LANES)
-    matrix, diag, g, q, r0, z, tx, ty, tz = call(
+    matrix, inverse, g, q, r0, w, z, tx, ty, tz = call(
         prepare,
-        (shape(EL, BLK, WIDE), vec, shape(3 * NV, 8, LANES), shape(3, 8, LANES, dtype=jnp.int32), vec, vec, tr, tr, tr),
+        (
+            shape(2, EL, BLK, WIDE),
+            vec,
+            shape(3 * NV, 8, LANES),
+            shape(3, 8, LANES, dtype=jnp.int32),
+            *[vec] * 3,
+            *[tr] * 3,
+        ),
         (
             vol_jac.reshape(EL, BLK, BLK),
             rhs.reshape(EL, BLK),
@@ -585,25 +640,31 @@
             orientation.reshape(EL, 6),
         ),
         scalar_args=(2,),
+        far_args=(0,),
+        scratch=[pltpu.VMEM((EL, BLK, BLK), jnp.float32), pltpu.SemaphoreType.DMA((EL,))],
     )
     basis, directions = [r0], [z]
     for iteration in range(ITERS):
         around = exchange(tx, ty)
-        part = call(own_part, vec, (matrix, diag, g, q, basis[-1], z, tz))
+        part = call(own_part, vec, (matrix, g, q, basis[-1], w, tz))
         if iteration < ITERS - 1:
-            r, z, tx, ty, tz = call(
-                advance, (vec, vec, tr, tr, tr), (side, part, *around, g, q, matrix, diag), scalar_args=(0,)
+            r, w, z, tx, ty, tz = call(
+                advance,
+                (vec, vec, vec, tr, tr, tr),
+                (part, *around, g, q, matrix, inverse),
             )
             basis.append(r)
             directions.append(z)
     total = nx * ny
-    sums = call(products, shape(total, LANES), (side, part, *around, g, q, *basis), scalar_args=(0,))
-    sums = lax.all_to_all(sums.reshape(total, 1, LANES), DEVICES_AXES, 0, 0).reshape(total, LANES)
-    update, ratio = call(finish, (shape(EL, BLK), tr), (sums, *directions))
-    fine = ratio[0, 1] > 0.5
+    sums = call(products, tr, (part, *around, g, q, *basis))
+    sums = jnp.broadcast_to(sums[0:1][None], (total, 1, LANES))
+    sums = lax.all_to_all(sums, DEVICES_AXES, 0, 0).reshape(total, LANES)
+    update, ratio, fine = call(
+        finish, (shape(EL, BLK), shape(1), shape(1, dtype=jnp.int32)), (sums, *directions), scalar_outs=(1, 2)
+    )
     return lax.cond(
-        fine,
-        lambda: (update.reshape(rhs.shape), ratio[0, 0]),
+        fine[0] == 1,
+        lambda: (update.reshape(rhs.shape), ratio[0]),
         lambda: careful(rhs, vol_jac, inv_step, face_jac, orientation),
     )
 

time: 68.2 us -> 62.2 us (0.912)
  Pallas kernels: 12.7 us -> 8.79 us
  waiting for transfers between devices: 15.7 us -> 14.2 us
    pallas_call x8, Pallas kernels: 12.7 us -> 8.79 us  [call(): pl.pallas_call(kernel, out_shape=outs, in_specs=in_specs, out_specs=out_s...]
    ppermute x12, waiting for transfers between devices: 2.95 us -> 1.29 us  [exchange(): lax.ppermute(tx if name.endswith('x') else ty, DEVICES_AXES, routes[name])]
    all_to_all x1, starting transfers between devices: 9.71 us -> 8.15 us  [body(): sums = lax.all_to_all(sums, DEVICES_AXES, 0, 0).reshape(total, LANES)]
    ppermute x12, starting transfers between devices: 25.2 us -> 26.5 us  [exchange(): lax.ppermute(tx if name.endswith('x') else ty, DEVICES_AXES, routes[name])]
    slice x2 -> x0, local copies, waits for them, and re-layouts: 1.09 us -> none  [the longest x1 0.58 us: body(): fine = ratio[0, 1] > 0.5]
    broadcast_in_dim x0 -> x2, local copies, waits for them, and re-layouts: none -> 0.73 us  [body(): sums = jnp.broadcast_to(sums[0:1][None], (total, 1, LANES))]
where the time goes in v2:
time: 62.2 us; the launch traced here: 62 us
  starting transfers between devices  34.6 us (56%)
  waiting for transfers between devices  14.2 us (23%)
  Pallas kernels  8.79 us (14%)
  between operations  2.64 us (4%)
  loops' own time  0.92 us (1%)
  local copies, waits for them, and re-layouts  0.75 us (1%)
    ppermute x12, starting transfers between devices, exchange(): lax.ppermute(tx if name.endswith('x') else ty, DEVICES_AXES, routes[name])  26.5 us
    all_to_all x1, waiting for transfers between devices, body(): sums = lax.all_to_all(sums, DEVICES_AXES, 0, 0).reshape(total, LANES)  12.9 us
    pallas_call x8, Pallas kernels, call(): pl.pallas_call(kernel, out_shape=outs, in_specs=in_specs, out_specs=out_s...  8.79 us
    all_to_all x1, starting transfers between devices, body(): sums = lax.all_to_all(sums, DEVICES_AXES, 0, 0).reshape(total, LANES)  8.15 us
    ppermute x12, waiting for transfers between devices, exchange(): lax.ppermute(tx if name.endswith('x') else ty, DEVICES_AXES, routes[name])  1.29 us
  transfers between devices with their start and end apart: 13, of which 4 were waited for; matrix products, arithmetic and copies ran while one was open for 0% of the time, Pallas kernels for 2%

profile of v2, /device:TPU:1, one launch (start us, length us, event | category | flops | bytes accessed | tf_op | source)
XLA Modules:
  0.0 62.0 jit_solution(12438721775882900282)
XLA Ops:
  0.6 4.0 %shard_map.92 = (f32[2,4,320,384]{3,2,1,0:T(8,128)S(1)}, f32[8,384]{1,0:T(8,128)S(1)}, f32[15,8,128]{2,1,0:T(8,128)S(1)}, s32[3,8,128]{2,1,0:T(8,128)S(1)}, f32[...) custom-call(f32[4,320,320]{2,1,0:T(8,128)} %bitcast.245, ...), custom_call_target="tpu_custom_call" | custom-call | tf_op jit(solution)/shard_map/pallas_call | solution.py:595
  4.7 3.1 %collective-permute-start.12 = (f32[8,128]{1,0:T(8,128)S(1)}, f32[8,128]{1,0:T(8,128)S(1)}, u32[]{:S(2)}, u32[]{:S(2)}) collective-permute-start(f32[8,128]{1,0:T(8,128)S(1)} %get-tuple-element.60), channel_id=1, source_target_pairs={{0,248},{1,249},{2,250},{3,251},{4,252},{5,253},{6,254},{7,255},{8... | collective-permute-start | bytes 12296 | tf_op jit(solution)/shard_map/ppermute | solution.py:621
  7.8 3.7 %collective-permute-start.13 = (f32[8,128]{1,0:T(8,128)S(1)}, f32[8,128]{1,0:T(8,128)S(1)}, u32[]{:S(2)}, u32[]{:S(2)}) collective-permute-start(f32[8,128]{1,0:T(8,128)S(1)} %get-tuple-element.61), channel_id=1, source_target_pairs={{0,7},{1,2},{2,1},{3,4},{4,3},{5,6},{6,5},{7,0},{8,15},{9,10},{10,... | collective-permute-start | bytes 12296 | tf_op jit(solution)/shard_map/ppermute | solution.py:621
  11.4 5.6 %collective-permute-start.15 = (f32[8,128]{1,0:T(8,128)S(1)}, f32[8,128]{1,0:T(8,128)S(1)}, u32[]{:S(2)}, u32[]{:S(2)}) collective-permute-start(f32[8,128]{1,0:T(8,128)S(1)} %get-tuple-element.60), channel_id=1, source_target_pairs={{0,8},{1,9},{2,10},{3,11},{4,12},{5,13},{6,14},{7,15},{8,0},{9,1},... | collective-permute-start | bytes 12296 | tf_op jit(solution)/shard_map/ppermute | solution.py:621
  17.1 0.4 shard_map.93.part_ref
  17.5 0.4 collective-permute-done.15.a3_ref
  17.9 1.3 %shard_map.94 = (f32[8,384]{1,0:T(8,128)S(1)}, f32[8,384]{1,0:T(8,128)S(1)}, f32[8,384]{1,0:T(8,128)S(1)}, f32[8,128]{1,0:T(8,128)S(1)}, f32[8,128]{1,0:T(8,128)S(1)}, /*index=5*/f32[8,128]{1,0:T(8,128)S(1)}) custom-call(f32[8,384]{1,0:T(8,128)S(1)} %shard_map.93.part_ref, f32[8,128]{1,0:T(8,128)S(1)} %collective-permute-done.12.a0_ref, ...), custom_call_target="tpu_custom_call" | custom-call | tf_op jit(solution)/shard_map/pallas_call | solution.py:595
  19.3 2.0 %collective-permute-start.17 = (f32[8,128]{1,0:T(8,128)S(1)}, f32[8,128]{1,0:T(8,128)S(1)}, u32[]{:S(2)}, u32[]{:S(2)}) collective-permute-start(f32[8,128]{1,0:T(8,128)S(1)} %get-tuple-element.67), channel_id=1, source_target_pairs={{0,7},{1,2},{2,1},{3,4},{4,3},{5,6},{6,5},{7,0},{8,15},{9,10},{10,... | collective-permute-start | bytes 12296 | tf_op jit(solution)/shard_map/ppermute | solution.py:621
  21.3 0.6 collective-permute-start.18
  21.8 3.3 %collective-permute-start.19 = (f32[8,128]{1,0:T(8,128)S(1)}, f32[8,128]{1,0:T(8,128)S(1)}, u32[]{:S(2)}, u32[]{:S(2)}) collective-permute-start(f32[8,128]{1,0:T(8,128)S(1)} %get-tuple-element.66), channel_id=1, source_target_pairs={{0,8},{1,9},{2,10},{3,11},{4,12},{5,13},{6,14},{7,15},{8,0},{9,1},... | collective-permute-start | bytes 12296 | tf_op jit(solution)/shard_map/ppermute | solution.py:621
  25.1 0.4 shard_map.95.part_ref
  25.5 0.4 collective-permute-done.19.a3_ref
  25.9 1.3 %shard_map.96 = (f32[8,384]{1,0:T(8,128)S(1)}, f32[8,384]{1,0:T(8,128)S(1)}, f32[8,384]{1,0:T(8,128)S(1)}, f32[8,128]{1,0:T(8,128)S(1)}, f32[8,128]{1,0:T(8,128)S(1)}, /*index=5*/f32[8,128]{1,0:T(8,128)S(1)}) custom-call(f32[8,384]{1,0:T(8,128)S(1)} %shard_map.95.part_ref, f32[8,128]{1,0:T(8,128)S(1)} %collective-permute-done.16.a0_ref, ...), custom_call_target="tpu_custom_call" | custom-call | tf_op jit(solution)/shard_map/pallas_call | solution.py:595
  27.2 1.0 %collective-permute-start.20 = (f32[8,128]{1,0:T(8,128)S(1)}, f32[8,128]{1,0:T(8,128)S(1)}, u32[]{:S(2)}, u32[]{:S(2)}) collective-permute-start(f32[8,128]{1,0:T(8,128)S(1)} %get-tuple-element.71), channel_id=1, source_target_pairs={{0,248},{1,249},{2,250},{3,251},{4,252},{5,253},{6,254},{7,255},{8... | collective-permute-start | bytes 12296 | tf_op jit(solution)/shard_map/ppermute | solution.py:621
  28.2 1.8 %collective-permute-start.21 = (f32[8,128]{1,0:T(8,128)S(1)}, f32[8,128]{1,0:T(8,128)S(1)}, u32[]{:S(2)}, u32[]{:S(2)}) collective-permute-start(f32[8,128]{1,0:T(8,128)S(1)} %get-tuple-element.72), channel_id=1, source_target_pairs={{0,7},{1,2},{2,1},{3,4},{4,3},{5,6},{6,5},{7,0},{8,15},{9,10},{10,... | collective-permute-start | bytes 12296 | tf_op jit(solution)/shard_map/ppermute | solution.py:621
  30.0 0.4 collective-permute-start.22
  30.4 5.1 %collective-permute-start.23 = (f32[8,128]{1,0:T(8,128)S(1)}, f32[8,128]{1,0:T(8,128)S(1)}, u32[]{:S(2)}, u32[]{:S(2)}) collective-permute-start(f32[8,128]{1,0:T(8,128)S(1)} %get-tuple-element.71), channel_id=1, source_target_pairs={{0,8},{1,9},{2,10},{3,11},{4,12},{5,13},{6,14},{7,15},{8,0},{9,1},... | collective-permute-start | bytes 12296 | tf_op jit(solution)/shard_map/ppermute | solution.py:621
  35.5 0.4 shard_map.97.part_ref
  35.9 0.4 collective-permute-done.23.a3_ref
  36.6 0.7 %broadcast_in_dim.7 = f32[256,1,128]{2,1,0:T(1,128)} broadcast(f32[128]{0:T(128)S(1)} %slice_bitcast_fusion), dimensions={2} | broadcast | bytes 131584 | tf_op jit(solution)/shard_map/broadcast_in_dim | solution.py:660
  37.3 8.1 %all-to-all-start = ((f32[256,1,128]{2,1,0:T(1,128)}), f32[256,1,128]{2,1,0:T(1,128)S(1)}, u32[]{:S(2)}, u32[]{:S(2)}) async-start(f32[256,1,128]{2,1,0:T(1,128)} %broadcast_in_dim.7), calls=%async_computation | async-start | bytes 262144 | tf_op jit(solution)/shard_map/all_to_all | solution.py:661
  45.4 12.9 %all-to-all-done = f32[256,1,128]{2,1,0:T(1,128)S(1)} async-done(((f32[256,1,128]{2,1,0:T(1,128)}), f32[256,1,128]{2,1,0:T(1,128)S(1)}, u32[]{:S(2)}, u32[]{:S(2)}) %all-to-all-start) | async-done | bytes 131104 | tf_op jit(solution)/shard_map/all_to_all | solution.py:661
  58.4 0.8 %shard_map.99 = (f32[4,320]{1,0:T(4,128)}, f32[1]{0:T(128)}, s32[1]{0:T(128)}) custom-call(f32[256,128]{1,0:T(8,128)S(1)} %bitcast.243, f32[8,384]{1,0:T(8,128)S(1)} %get-tuple-element.73.z1_ref, f32[8,384]{1,0:T(8,128)S(1)} %get-tuple-element.74.z2_ref, f32[8,384]{1,0:T(8,128)S(1)} %get-tuple-element.75.z3_ref), custom_call_target="tpu_custom_call" | custom-call | tf_op jit(solution)/shard_map/pallas_call | solution.py:595
  59.9 0.9 %conditional.1 = (f32[1,1,4,320]{3,2,1,0:T(4,128)}, f32[]{:T(128)}) conditional(s32[]{:T(128)} %bitcast.85, (f32[1,1,4]{2,1,0:T(1,128)S(1)}, (), f32[1,1,4,6,5,5]{3,2,5,4,1,0:T(4,128)S(1)}, f32[1,1,4,320,320]{4,3,2,1,0:T(8,128)S(1)}, f32[1,1,4,320]{3,2,1,0:T(4,128)S(1)}, /*index=5*/s32[1,1,4,6]{3,2,1,0:T(4,128)S(1)}, ()) %tuple.54, ...), branch_computations={%region_0.22_spmd, %region_22.23_spmd} | conditional | flops 9523977216 | bytes 61447376 | solution.py:665
  (23 shorter events, 0.4 us)
Async XLA Ops:
  4.7 12.8 %collective-permute-start.12 = (f32[8,128]{1,0:T(8,128)S(1)}, f32[8,128]{1,0:T(8,128)S(1)}, u32[]{:S(2)}, u32[]{:S(2)}) collective-permute-start(f32[8,128]{1,0:T(8,128)S(1)} %get-tuple-element.60), channel_id=1, source_target_pairs={{0,248},{1,249},{2,250},{3,251},{4,252},{5,253},{6,254},{7,255},{8... | collective-permute-start | bytes 12296 | tf_op jit(solution)/shard_map/ppermute | solution.py:621
  7.8 9.7 %collective-permute-start.13 = (f32[8,128]{1,0:T(8,128)S(1)}, f32[8,128]{1,0:T(8,128)S(1)}, u32[]{:S(2)}, u32[]{:S(2)}) collective-permute-start(f32[8,128]{1,0:T(8,128)S(1)} %get-tuple-element.61), channel_id=1, source_target_pairs={{0,7},{1,2},{2,1},{3,4},{4,3},{5,6},{6,5},{7,0},{8,15},{9,10},{10,... | collective-permute-start | bytes 12296 | tf_op jit(solution)/shard_map/ppermute | solution.py:621
  11.4 6.0 %collective-permute-start.14 = (f32[8,128]{1,0:T(8,128)S(1)}, f32[8,128]{1,0:T(8,128)S(1)}, u32[]{:S(2)}, u32[]{:S(2)}) collective-permute-start(f32[8,128]{1,0:T(8,128)S(1)} %get-tuple-element.61), channel_id=1, source_target_pairs={{0,1},{1,0},{2,3},{3,2},{4,5},{5,4},{6,7},{7,6},{8,9},{9,8},{10,11... | collective-permute-start | bytes 12296 | tf_op jit(solution)/shard_map/ppermute | solution.py:621
  11.4 6.4 %collective-permute-start.15 = (f32[8,128]{1,0:T(8,128)S(1)}, f32[8,128]{1,0:T(8,128)S(1)}, u32[]{:S(2)}, u32[]{:S(2)}) collective-permute-start(f32[8,128]{1,0:T(8,128)S(1)} %get-tuple-element.60), channel_id=1, source_target_pairs={{0,8},{1,9},{2,10},{3,11},{4,12},{5,13},{6,14},{7,15},{8,0},{9,1},... | collective-permute-start | bytes 12296 | tf_op jit(solution)/shard_map/ppermute | solution.py:621
  19.2 6.3 %collective-permute-start.16 = (f32[8,128]{1,0:T(8,128)S(1)}, f32[8,128]{1,0:T(8,128)S(1)}, u32[]{:S(2)}, u32[]{:S(2)}) collective-permute-start(f32[8,128]{1,0:T(8,128)S(1)} %get-tuple-element.66), channel_id=1, source_target_pairs={{0,248},{1,249},{2,250},{3,251},{4,252},{5,253},{6,254},{7,255},{8... | collective-permute-start | bytes 12296 | tf_op jit(solution)/shard_map/ppermute | solution.py:621
  19.3 6.2 %collective-permute-start.17 = (f32[8,128]{1,0:T(8,128)S(1)}, f32[8,128]{1,0:T(8,128)S(1)}, u32[]{:S(2)}, u32[]{:S(2)}) collective-permute-start(f32[8,128]{1,0:T(8,128)S(1)} %get-tuple-element.67), channel_id=1, source_target_pairs={{0,7},{1,2},{2,1},{3,4},{4,3},{5,6},{6,5},{7,0},{8,15},{9,10},{10,... | collective-permute-start | bytes 12296 | tf_op jit(solution)/shard_map/ppermute | solution.py:621
  21.3 4.2 %collective-permute-start.18 = (f32[8,128]{1,0:T(8,128)S(1)}, f32[8,128]{1,0:T(8,128)S(1)}, u32[]{:S(2)}, u32[]{:S(2)}) collective-permute-start(f32[8,128]{1,0:T(8,128)S(1)} %get-tuple-element.67), channel_id=1, source_target_pairs={{0,1},{1,0},{2,3},{3,2},{4,5},{5,4},{6,7},{7,6},{8,9},{9,8},{10,11... | collective-permute-start | bytes 12296 | tf_op jit(solution)/shard_map/ppermute | solution.py:621
  21.8 4.1 %collective-permute-start.19 = (f32[8,128]{1,0:T(8,128)S(1)}, f32[8,128]{1,0:T(8,128)S(1)}, u32[]{:S(2)}, u32[]{:S(2)}) collective-permute-start(f32[8,128]{1,0:T(8,128)S(1)} %get-tuple-element.66), channel_id=1, source_target_pairs={{0,8},{1,9},{2,10},{3,11},{4,12},{5,13},{6,14},{7,15},{8,0},{9,1},... | collective-permute-start | bytes 12296 | tf_op jit(solution)/shard_map/ppermute | solution.py:621
  27.2 8.6 %collective-permute-start.20 = (f32[8,128]{1,0:T(8,128)S(1)}, f32[8,128]{1,0:T(8,128)S(1)}, u32[]{:S(2)}, u32[]{:S(2)}) collective-permute-start(f32[8,128]{1,0:T(8,128)S(1)} %get-tuple-element.71), channel_id=1, source_target_pairs={{0,248},{1,249},{2,250},{3,251},{4,252},{5,253},{6,254},{7,255},{8... | collective-permute-start | bytes 12296 | tf_op jit(solution)/shard_map/ppermute | solution.py:621
  28.2 7.7 %collective-permute-start.21 = (f32[8,128]{1,0:T(8,128)S(1)}, f32[8,128]{1,0:T(8,128)S(1)}, u32[]{:S(2)}, u32[]{:S(2)}) collective-permute-start(f32[8,128]{1,0:T(8,128)S(1)} %get-tuple-element.72), channel_id=1, source_target_pairs={{0,7},{1,2},{2,1},{3,4},{4,3},{5,6},{6,5},{7,0},{8,15},{9,10},{10,... | collective-permute-start | bytes 12296 | tf_op jit(solution)/shard_map/ppermute | solution.py:621
  30.0 5.9 %collective-permute-start.22 = (f32[8,128]{1,0:T(8,128)S(1)}, f32[8,128]{1,0:T(8,128)S(1)}, u32[]{:S(2)}, u32[]{:S(2)}) collective-permute-start(f32[8,128]{1,0:T(8,128)S(1)} %get-tuple-element.72), channel_id=1, source_target_pairs={{0,1},{1,0},{2,3},{3,2},{4,5},{5,4},{6,7},{7,6},{8,9},{9,8},{10,11... | collective-permute-start | bytes 12296 | tf_op jit(solution)/shard_map/ppermute | solution.py:621
  30.4 5.9 %collective-permute-start.23 = (f32[8,128]{1,0:T(8,128)S(1)}, f32[8,128]{1,0:T(8,128)S(1)}, u32[]{:S(2)}, u32[]{:S(2)}) collective-permute-start(f32[8,128]{1,0:T(8,128)S(1)} %get-tuple-element.71), channel_id=1, source_target_pairs={{0,8},{1,9},{2,10},{3,11},{4,12},{5,13},{6,14},{7,15},{8,0},{9,1},... | collective-permute-start | bytes 12296 | tf_op jit(solution)/shard_map/ppermute | solution.py:621
  35.5 24.4 %copy-start = (f32[1,1,4,320,320]{4,3,2,1,0:T(8,128)S(1)}, f32[1,1,4,320,320]{4,3,2,1,0:T(8,128)}, u32[]{:S(2)}) copy-start(f32[1,1,4,320,320]{4,3,2,1,0:T(8,128)} %param.10) | copy-start | bytes 4915204
  35.5 24.4 %copy-start.2 = (f32[1,1,4,320]{3,2,1,0:T(4,128)S(1)}, f32[1,1,4,320]{3,2,1,0:T(4,128)}, u32[]{:S(2)}) copy-start(f32[1,1,4,320]{3,2,1,0:T(4,128)} %param.9) | copy-start | bytes 15364
  35.5 24.4 %copy-start.6 = (f32[1,1,4,6,5,5]{3,2,5,4,1,0:T(4,128)S(1)}, f32[1,1,4,6,5,5]{3,2,5,4,1,0:T(4,128)}, u32[]{:S(2)}) copy-start(f32[1,1,4,6,5,5]{3,2,5,4,1,0:T(4,128)} %param.12) | copy-start | bytes 7204
  35.5 24.4 %copy-start.8 = (f32[1,1,4]{2,1,0:T(1,128)S(1)}, f32[1,1,4]{2,1,0:T(1,128)}, u32[]{:S(2)}) copy-start(f32[1,1,4]{2,1,0:T(1,128)} %param.11) | copy-start | bytes 52
  35.5 24.4 %copy-start.9 = (s32[1,1,4,6]{3,2,1,0:T(4,128)S(1)}, s32[1,1,4,6]{3,2,1,0:T(4,128)}, u32[]{:S(2)}) copy-start(s32[1,1,4,6]{3,2,1,0:T(4,128)} %param.13) | copy-start | bytes 292
  37.3 21.1 %all-to-all-start = ((f32[256,1,128]{2,1,0:T(1,128)}), f32[256,1,128]{2,1,0:T(1,128)S(1)}, u32[]{:S(2)}, u32[]{:S(2)}) async-start(f32[256,1,128]{2,1,0:T(1,128)} %broadcast_in_dim.7), calls=%async_computation | async-start | bytes 262144 | tf_op jit(solution)/shard_map/all_to_all | solution.py:661

commit v3 on v2

--- a/solution.py
+++ b/solution.py
@@ -206,7 +206,7 @@
 MIN_SCALE = 1e-18
 MAX_SCALE = 1e30
 DEVICES_AXES = ("gx", "gy")
-ROUTE_ORDER = ("far x", "far y", "near y", "near x")
+ROUTE_ORDER = ("near x", "far x", "far y", "near y")
 
 
 def tile_iota(dim):

time: 62.2 us -> 63 us (1.013)
  waiting for transfers between devices: 14.2 us -> 20 us
  starting transfers between devices: 34.6 us -> 29.7 us
    ppermute x12, starting transfers between devices: 26.5 us -> 20.7 us  [exchange(): lax.ppermute(tx if name.endswith('x') else ty, DEVICES_AXES, routes[name])]
    ppermute x12, waiting for transfers between devices: 1.29 us -> 7.09 us  [exchange(): lax.ppermute(tx if name.endswith('x') else ty, DEVICES_AXES, routes[name])]
    all_to_all x1, starting transfers between devices: 8.15 us -> 9.06 us  [body(): sums = lax.all_to_all(sums, DEVICES_AXES, 0, 0).reshape(total, LANES)]
  transfers between devices with their start and end apart: 13 -> 13, of which waited for: 4 -> 7; matrix products, arithmetic and copies ran while one was open for 0% -> 0% of each run, Pallas kernels for 2% -> 2%
where the time goes in v3:
time: 63 us; the launch traced here: 62.8 us
  starting transfers between devices  29.7 us (47%)
  waiting for transfers between devices  20 us (32%)
  Pallas kernels  8.8 us (14%)
  between operations  2.6 us (4%)
  loops' own time  0.92 us (1%)
  local copies, waits for them, and re-layouts  0.75 us (1%)
    ppermute x12, starting transfers between devices, exchange(): lax.ppermute(tx if name.endswith('x') else ty, DEVICES_AXES, routes[name])  20.7 us
    all_to_all x1, waiting for transfers between devices, body(): sums = lax.all_to_all(sums, DEVICES_AXES, 0, 0).reshape(total, LANES)  12.9 us
    all_to_all x1, starting transfers between devices, body(): sums = lax.all_to_all(sums, DEVICES_AXES, 0, 0).reshape(total, LANES)  9.06 us
    pallas_call x8, Pallas kernels, call(): pl.pallas_call(kernel, out_shape=outs, in_specs=in_specs, out_specs=out_s...  8.8 us
    ppermute x12, waiting for transfers between devices, exchange(): lax.ppermute(tx if name.endswith('x') else ty, DEVICES_AXES, routes[name])  7.09 us
  transfers between devices with their start and end apart: 13, of which 7 were waited for; matrix products, arithmetic and copies ran while one was open for 0% of the time, Pallas kernels for 2%

profile of v3, /device:TPU:1, one launch (start us, length us, event | category | flops | bytes accessed | tf_op | source)
XLA Modules:
  0.0 62.8 jit_solution(8185199401704952154)
XLA Ops:
  0.6 4.0 %shard_map.92 = (f32[2,4,320,384]{3,2,1,0:T(8,128)S(1)}, f32[8,384]{1,0:T(8,128)S(1)}, f32[15,8,128]{2,1,0:T(8,128)S(1)}, s32[3,8,128]{2,1,0:T(8,128)S(1)}, f32[...) custom-call(f32[4,320,320]{2,1,0:T(8,128)} %bitcast.245, ...), custom_call_target="tpu_custom_call" | custom-call | tf_op jit(solution)/shard_map/pallas_call | solution.py:595
  4.7 3.3 %collective-permute-start.12 = (f32[8,128]{1,0:T(8,128)S(1)}, f32[8,128]{1,0:T(8,128)S(1)}, u32[]{:S(2)}, u32[]{:S(2)}) collective-permute-start(f32[8,128]{1,0:T(8,128)S(1)} %get-tuple-element.60), channel_id=1, source_target_pairs={{0,8},{1,9},{2,10},{3,11},{4,12},{5,13},{6,14},{7,15},{8,0},{9,1},... | collective-permute-start | bytes 12296 | tf_op jit(solution)/shard_map/ppermute | solution.py:621
  8.0 3.5 %collective-permute-start.14 = (f32[8,128]{1,0:T(8,128)S(1)}, f32[8,128]{1,0:T(8,128)S(1)}, u32[]{:S(2)}, u32[]{:S(2)}) collective-permute-start(f32[8,128]{1,0:T(8,128)S(1)} %get-tuple-element.61), channel_id=1, source_target_pairs={{0,7},{1,2},{2,1},{3,4},{4,3},{5,6},{6,5},{7,0},{8,15},{9,10},{10,... | collective-permute-start | bytes 12296 | tf_op jit(solution)/shard_map/ppermute | solution.py:621
  11.5 0.4 shard_map.93.part_ref
  11.9 0.6 %collective-permute-done.14.a2_ref = f32[8,128]{1,0:T(8,128)S(1)} collective-permute-done((f32[8,128]{1,0:T(8,128)S(1)}, f32[8,128]{1,0:T(8,128)S(1)}, u32[]{:S(2)}, u32[]{:S(2)}) %collective-permute-start.14) | collective-permute-done | bytes 4128 | tf_op jit(solution)/shard_map/ppermute | solution.py:621
  12.6 1.7 %collective-permute-done.15.a3_ref = f32[8,128]{1,0:T(8,128)S(1)} collective-permute-done((f32[8,128]{1,0:T(8,128)S(1)}, f32[8,128]{1,0:T(8,128)S(1)}, u32[]{:S(2)}, u32[]{:S(2)}) %collective-permute-start.15) | collective-permute-done | bytes 4128 | tf_op jit(solution)/shard_map/ppermute | solution.py:621
  14.3 1.3 %shard_map.94 = (f32[8,384]{1,0:T(8,128)S(1)}, f32[8,384]{1,0:T(8,128)S(1)}, f32[8,384]{1,0:T(8,128)S(1)}, f32[8,128]{1,0:T(8,128)S(1)}, f32[8,128]{1,0:T(8,128)S(1)}, /*index=5*/f32[8,128]{1,0:T(8,128)S(1)}) custom-call(f32[8,384]{1,0:T(8,128)S(1)} %shard_map.93.part_ref, f32[8,128]{1,0:T(8,128)S(1)} %collective-permute-done.12.a0_ref, ...), custom_call_target="tpu_custom_call" | custom-call | tf_op jit(solution)/shard_map/pallas_call | solution.py:595
  15.6 7.1 %collective-permute-start.16 = (f32[8,128]{1,0:T(8,128)S(1)}, f32[8,128]{1,0:T(8,128)S(1)}, u32[]{:S(2)}, u32[]{:S(2)}) collective-permute-start(f32[8,128]{1,0:T(8,128)S(1)} %get-tuple-element.66), channel_id=1, source_target_pairs={{0,8},{1,9},{2,10},{3,11},{4,12},{5,13},{6,14},{7,15},{8,0},{9,1},... | collective-permute-start | bytes 12296 | tf_op jit(solution)/shard_map/ppermute | solution.py:621
  22.7 1.8 %collective-permute-start.18 = (f32[8,128]{1,0:T(8,128)S(1)}, f32[8,128]{1,0:T(8,128)S(1)}, u32[]{:S(2)}, u32[]{:S(2)}) collective-permute-start(f32[8,128]{1,0:T(8,128)S(1)} %get-tuple-element.67), channel_id=1, source_target_pairs={{0,7},{1,2},{2,1},{3,4},{4,3},{5,6},{6,5},{7,0},{8,15},{9,10},{10,... | collective-permute-start | bytes 12296 | tf_op jit(solution)/shard_map/ppermute | solution.py:621
  24.6 0.4 shard_map.95.part_ref
  24.9 0.8 %collective-permute-done.17.a1_ref = f32[8,128]{1,0:T(8,128)S(1)} collective-permute-done((f32[8,128]{1,0:T(8,128)S(1)}, f32[8,128]{1,0:T(8,128)S(1)}, u32[]{:S(2)}, u32[]{:S(2)}) %collective-permute-start.17) | collective-permute-done | bytes 4128 | tf_op jit(solution)/shard_map/ppermute | solution.py:621
  25.8 1.5 %collective-permute-done.18.a2_ref = f32[8,128]{1,0:T(8,128)S(1)} collective-permute-done((f32[8,128]{1,0:T(8,128)S(1)}, f32[8,128]{1,0:T(8,128)S(1)}, u32[]{:S(2)}, u32[]{:S(2)}) %collective-permute-start.18) | collective-permute-done | bytes 4128 | tf_op jit(solution)/shard_map/ppermute | solution.py:621
  27.3 1.3 %shard_map.96 = (f32[8,384]{1,0:T(8,128)S(1)}, f32[8,384]{1,0:T(8,128)S(1)}, f32[8,384]{1,0:T(8,128)S(1)}, f32[8,128]{1,0:T(8,128)S(1)}, f32[8,128]{1,0:T(8,128)S(1)}, /*index=5*/f32[8,128]{1,0:T(8,128)S(1)}) custom-call(f32[8,384]{1,0:T(8,128)S(1)} %shard_map.95.part_ref, f32[8,128]{1,0:T(8,128)S(1)} %collective-permute-done.16.a0_ref, ...), custom_call_target="tpu_custom_call" | custom-call | tf_op jit(solution)/shard_map/pallas_call | solution.py:595
  28.6 2.9 %collective-permute-start.20 = (f32[8,128]{1,0:T(8,128)S(1)}, f32[8,128]{1,0:T(8,128)S(1)}, u32[]{:S(2)}, u32[]{:S(2)}) collective-permute-start(f32[8,128]{1,0:T(8,128)S(1)} %get-tuple-element.71), channel_id=1, source_target_pairs={{0,8},{1,9},{2,10},{3,11},{4,12},{5,13},{6,14},{7,15},{8,0},{9,1},... | collective-permute-start | bytes 12296 | tf_op jit(solution)/shard_map/ppermute | solution.py:621
  31.7 1.8 %collective-permute-start.22 = (f32[8,128]{1,0:T(8,128)S(1)}, f32[8,128]{1,0:T(8,128)S(1)}, u32[]{:S(2)}, u32[]{:S(2)}) collective-permute-start(f32[8,128]{1,0:T(8,128)S(1)} %get-tuple-element.72), channel_id=1, source_target_pairs={{0,7},{1,2},{2,1},{3,4},{4,3},{5,6},{6,5},{7,0},{8,15},{9,10},{10,... | collective-permute-start | bytes 12296 | tf_op jit(solution)/shard_map/ppermute | solution.py:621
  33.5 0.4 shard_map.97.part_ref
  33.9 0.7 %collective-permute-done.21.a1_ref = f32[8,128]{1,0:T(8,128)S(1)} collective-permute-done((f32[8,128]{1,0:T(8,128)S(1)}, f32[8,128]{1,0:T(8,128)S(1)}, u32[]{:S(2)}, u32[]{:S(2)}) %collective-permute-start.21) | collective-permute-done | bytes 4128 | tf_op jit(solution)/shard_map/ppermute | solution.py:621
  34.6 1.7 %collective-permute-done.22.a2_ref = f32[8,128]{1,0:T(8,128)S(1)} collective-permute-done((f32[8,128]{1,0:T(8,128)S(1)}, f32[8,128]{1,0:T(8,128)S(1)}, u32[]{:S(2)}, u32[]{:S(2)}) %collective-permute-start.22) | collective-permute-done | bytes 4128 | tf_op jit(solution)/shard_map/ppermute | solution.py:621
  36.3 0.3 shard_map.98
  36.5 0.7 %broadcast_in_dim.7 = f32[256,1,128]{2,1,0:T(1,128)} broadcast(f32[128]{0:T(128)S(1)} %slice_bitcast_fusion), dimensions={2} | broadcast | bytes 131584 | tf_op jit(solution)/shard_map/broadcast_in_dim | solution.py:660
  37.2 9.1 %all-to-all-start = ((f32[256,1,128]{2,1,0:T(1,128)}), f32[256,1,128]{2,1,0:T(1,128)S(1)}, u32[]{:S(2)}, u32[]{:S(2)}) async-start(f32[256,1,128]{2,1,0:T(1,128)} %broadcast_in_dim.7), calls=%async_computation | async-start | bytes 262144 | tf_op jit(solution)/shard_map/all_to_all | solution.py:661
  46.3 12.9 %all-to-all-done = f32[256,1,128]{2,1,0:T(1,128)S(1)} async-done(((f32[256,1,128]{2,1,0:T(1,128)}), f32[256,1,128]{2,1,0:T(1,128)S(1)}, u32[]{:S(2)}, u32[]{:S(2)}) %all-to-all-start) | async-done | bytes 131104 | tf_op jit(solution)/shard_map/all_to_all | solution.py:661
  59.2 0.8 %shard_map.99 = (f32[4,320]{1,0:T(4,128)}, f32[1]{0:T(128)}, s32[1]{0:T(128)}) custom-call(f32[256,128]{1,0:T(8,128)S(1)} %bitcast.243, f32[8,384]{1,0:T(8,128)S(1)} %get-tuple-element.73.z1_ref, f32[8,384]{1,0:T(8,128)S(1)} %get-tuple-element.74.z2_ref, f32[8,384]{1,0:T(8,128)S(1)} %get-tuple-element.75.z3_ref), custom_call_target="tpu_custom_call" | custom-call | tf_op jit(solution)/shard_map/pallas_call | solution.py:595
  60.8 0.9 %conditional.1 = (f32[1,1,4,320]{3,2,1,0:T(4,128)}, f32[]{:T(128)}) conditional(s32[]{:T(128)} %bitcast.85, (f32[1,1,4]{2,1,0:T(1,128)S(1)}, (), f32[1,1,4,6,5,5]{3,2,5,4,1,0:T(4,128)S(1)}, f32[1,1,4,320,320]{4,3,2,1,0:T(8,128)S(1)}, f32[1,1,4,320]{3,2,1,0:T(4,128)S(1)}, /*index=5*/s32[1,1,4,6]{3,2,1,0:T(4,128)S(1)}, ()) %tuple.54, ...), branch_computations={%region_0.22_spmd, %region_22.23_spmd} | conditional | flops 9523977216 | bytes 61447376 | solution.py:665
  (23 shorter events, 0.2 us)
Async XLA Ops:
  4.7 7.2 %collective-permute-start.12 = (f32[8,128]{1,0:T(8,128)S(1)}, f32[8,128]{1,0:T(8,128)S(1)}, u32[]{:S(2)}, u32[]{:S(2)}) collective-permute-start(f32[8,128]{1,0:T(8,128)S(1)} %get-tuple-element.60), channel_id=1, source_target_pairs={{0,8},{1,9},{2,10},{3,11},{4,12},{5,13},{6,14},{7,15},{8,0},{9,1},... | collective-permute-start | bytes 12296 | tf_op jit(solution)/shard_map/ppermute | solution.py:621
  8.0 3.9 %collective-permute-start.13 = (f32[8,128]{1,0:T(8,128)S(1)}, f32[8,128]{1,0:T(8,128)S(1)}, u32[]{:S(2)}, u32[]{:S(2)}) collective-permute-start(f32[8,128]{1,0:T(8,128)S(1)} %get-tuple-element.60), channel_id=1, source_target_pairs={{0,248},{1,249},{2,250},{3,251},{4,252},{5,253},{6,254},{7,255},{8... | collective-permute-start | bytes 12296 | tf_op jit(solution)/shard_map/ppermute | solution.py:621
  8.0 4.6 %collective-permute-start.14 = (f32[8,128]{1,0:T(8,128)S(1)}, f32[8,128]{1,0:T(8,128)S(1)}, u32[]{:S(2)}, u32[]{:S(2)}) collective-permute-start(f32[8,128]{1,0:T(8,128)S(1)} %get-tuple-element.61), channel_id=1, source_target_pairs={{0,7},{1,2},{2,1},{3,4},{4,3},{5,6},{6,5},{7,0},{8,15},{9,10},{10,... | collective-permute-start | bytes 12296 | tf_op jit(solution)/shard_map/ppermute | solution.py:621
  11.5 2.8 %collective-permute-start.15 = (f32[8,128]{1,0:T(8,128)S(1)}, f32[8,128]{1,0:T(8,128)S(1)}, u32[]{:S(2)}, u32[]{:S(2)}) collective-permute-start(f32[8,128]{1,0:T(8,128)S(1)} %get-tuple-element.61), channel_id=1, source_target_pairs={{0,1},{1,0},{2,3},{3,2},{4,5},{5,4},{6,7},{7,6},{8,9},{9,8},{10,11... | collective-permute-start | bytes 12296 | tf_op jit(solution)/shard_map/ppermute | solution.py:621
  15.6 9.3 %collective-permute-start.16 = (f32[8,128]{1,0:T(8,128)S(1)}, f32[8,128]{1,0:T(8,128)S(1)}, u32[]{:S(2)}, u32[]{:S(2)}) collective-permute-start(f32[8,128]{1,0:T(8,128)S(1)} %get-tuple-element.66), channel_id=1, source_target_pairs={{0,8},{1,9},{2,10},{3,11},{4,12},{5,13},{6,14},{7,15},{8,0},{9,1},... | collective-permute-start | bytes 12296 | tf_op jit(solution)/shard_map/ppermute | solution.py:621
  22.7 3.0 %collective-permute-start.17 = (f32[8,128]{1,0:T(8,128)S(1)}, f32[8,128]{1,0:T(8,128)S(1)}, u32[]{:S(2)}, u32[]{:S(2)}) collective-permute-start(f32[8,128]{1,0:T(8,128)S(1)} %get-tuple-element.66), channel_id=1, source_target_pairs={{0,248},{1,249},{2,250},{3,251},{4,252},{5,253},{6,254},{7,255},{8... | collective-permute-start | bytes 12296 | tf_op jit(solution)/shard_map/ppermute | solution.py:621
  22.7 4.6 %collective-permute-start.18 = (f32[8,128]{1,0:T(8,128)S(1)}, f32[8,128]{1,0:T(8,128)S(1)}, u32[]{:S(2)}, u32[]{:S(2)}) collective-permute-start(f32[8,128]{1,0:T(8,128)S(1)} %get-tuple-element.67), channel_id=1, source_target_pairs={{0,7},{1,2},{2,1},{3,4},{4,3},{5,6},{6,5},{7,0},{8,15},{9,10},{10,... | collective-permute-start | bytes 12296 | tf_op jit(solution)/shard_map/ppermute | solution.py:621
  24.6 2.8 %collective-permute-start.19 = (f32[8,128]{1,0:T(8,128)S(1)}, f32[8,128]{1,0:T(8,128)S(1)}, u32[]{:S(2)}, u32[]{:S(2)}) collective-permute-start(f32[8,128]{1,0:T(8,128)S(1)} %get-tuple-element.67), channel_id=1, source_target_pairs={{0,1},{1,0},{2,3},{3,2},{4,5},{5,4},{6,7},{7,6},{8,9},{9,8},{10,11... | collective-permute-start | bytes 12296 | tf_op jit(solution)/shard_map/ppermute | solution.py:621
  28.6 5.3 %collective-permute-start.20 = (f32[8,128]{1,0:T(8,128)S(1)}, f32[8,128]{1,0:T(8,128)S(1)}, u32[]{:S(2)}, u32[]{:S(2)}) collective-permute-start(f32[8,128]{1,0:T(8,128)S(1)} %get-tuple-element.71), channel_id=1, source_target_pairs={{0,8},{1,9},{2,10},{3,11},{4,12},{5,13},{6,14},{7,15},{8,0},{9,1},... | collective-permute-start | bytes 12296 | tf_op jit(solution)/shard_map/ppermute | solution.py:621
  31.5 3.0 %collective-permute-start.21 = (f32[8,128]{1,0:T(8,128)S(1)}, f32[8,128]{1,0:T(8,128)S(1)}, u32[]{:S(2)}, u32[]{:S(2)}) collective-permute-start(f32[8,128]{1,0:T(8,128)S(1)} %get-tuple-element.71), channel_id=1, source_target_pairs={{0,248},{1,249},{2,250},{3,251},{4,252},{5,253},{6,254},{7,255},{8... | collective-permute-start | bytes 12296 | tf_op jit(solution)/shard_map/ppermute | solution.py:621
  31.7 4.6 %collective-permute-start.22 = (f32[8,128]{1,0:T(8,128)S(1)}, f32[8,128]{1,0:T(8,128)S(1)}, u32[]{:S(2)}, u32[]{:S(2)}) collective-permute-start(f32[8,128]{1,0:T(8,128)S(1)} %get-tuple-element.72), channel_id=1, source_target_pairs={{0,7},{1,2},{2,1},{3,4},{4,3},{5,6},{6,5},{7,0},{8,15},{9,10},{10,... | collective-permute-start | bytes 12296 | tf_op jit(solution)/shard_map/ppermute | solution.py:621
  33.5 2.8 %collective-permute-start.23 = (f32[8,128]{1,0:T(8,128)S(1)}, f32[8,128]{1,0:T(8,128)S(1)}, u32[]{:S(2)}, u32[]{:S(2)}) collective-permute-start(f32[8,128]{1,0:T(8,128)S(1)} %get-tuple-element.72), channel_id=1, source_target_pairs={{0,1},{1,0},{2,3},{3,2},{4,5},{5,4},{6,7},{7,6},{8,9},{9,8},{10,11... | collective-permute-start | bytes 12296 | tf_op jit(solution)/shard_map/ppermute | solution.py:621
  33.5 27.2 %copy-start = (f32[1,1,4,320,320]{4,3,2,1,0:T(8,128)S(1)}, f32[1,1,4,320,320]{4,3,2,1,0:T(8,128)}, u32[]{:S(2)}) copy-start(f32[1,1,4,320,320]{4,3,2,1,0:T(8,128)} %param.10) | copy-start | bytes 4915204
  33.5 27.2 %copy-start.2 = (f32[1,1,4,320]{3,2,1,0:T(4,128)S(1)}, f32[1,1,4,320]{3,2,1,0:T(4,128)}, u32[]{:S(2)}) copy-start(f32[1,1,4,320]{3,2,1,0:T(4,128)} %param.9) | copy-start | bytes 15364
  33.5 27.2 %copy-start.6 = (f32[1,1,4,6,5,5]{3,2,5,4,1,0:T(4,128)S(1)}, f32[1,1,4,6,5,5]{3,2,5,4,1,0:T(4,128)}, u32[]{:S(2)}) copy-start(f32[1,1,4,6,5,5]{3,2,5,4,1,0:T(4,128)} %param.12) | copy-start | bytes 7204
  33.5 27.2 %copy-start.8 = (f32[1,1,4]{2,1,0:T(1,128)S(1)}, f32[1,1,4]{2,1,0:T(1,128)}, u32[]{:S(2)}) copy-start(f32[1,1,4]{2,1,0:T(1,128)} %param.11) | copy-start | bytes 52
  33.5 27.2 %copy-start.9 = (s32[1,1,4,6]{3,2,1,0:T(4,128)S(1)}, s32[1,1,4,6]{3,2,1,0:T(4,128)}, u32[]{:S(2)}) copy-start(s32[1,1,4,6]{3,2,1,0:T(4,128)} %param.13) | copy-start | bytes 292
  37.2 22.0 %all-to-all-start = ((f32[256,1,128]{2,1,0:T(1,128)}), f32[256,1,128]{2,1,0:T(1,128)S(1)}, u32[]{:S(2)}, u32[]{:S(2)}) async-start(f32[256,1,128]{2,1,0:T(1,128)} %broadcast_in_dim.7), calls=%async_computation | async-start | bytes 262144 | tf_op jit(solution)/shard_map/all_to_all | solution.py:661
